TPU v7x, 512 devices: a whole 4x4x16 slice. The times are simulated.
512 devices in a mesh: section: 16 (over y, x), expert: 32 (over z, core).
Axes of the slice: x: 4, y: 4, z: 16, core: 2. Of those that a mesh axis runs over, the one named last changes fastest.
Arguments:
- grad_in: bfloat16 [16, 2, 1024, 3584], P('section', None, 'expert'), may hold values from -6 to 6
- fresh_grad: bfloat16 [2, 1024, 3584], P(None, 'expert'), may hold values from -6 to 6
- routes: int32 [16, 2, 2, 1024, 2], P('section', None, None, 'expert'), may hold values from 0 to 7, all different within a row; in each aligned block of 32 rows (0 to 31, 32 to 63, ..., all dimensions but the last counted through in order) at most 12 rows name the same one
- gate_weights: bfloat16 [16, 2, 2, 1024, 2], P('section', None, None, 'expert'), may hold values from 0.099609375 to 1
- saved_pre: bfloat16 [16, 2, 2, 384, 8192], P('section', None, None, None, 'expert'), may hold values from -6 to 6
- w_up: bfloat16 [16, 3584, 8192], P('section', None, 'expert'), may hold values from -0.1875 to 0.1875
- w_down: bfloat16 [16, 8192, 3584], P('section', 'expert'), may hold values from -0.09375 to 0.09375
Outputs:
- grad_out: bfloat16 [16, 2, 1024, 3584], P('section', None, 'expert')
Inputs may be any that keep to these rules, and one draw needn't show every extreme that they name: `routes`: each token names 2 different experts. Among the 32 tokens of one device no expert is named more than 12 times, and in every draw some device names some expert exactly 12 times.
All inputs are finite; a program needn't handle non-finite values.
Results may differ from a plain program's by a relative error of at most 0.011.
Values may be sent and summed in bfloat16 or wider, within the bound.
No kernel may reach another device: no remote copies, remote signals or barrier semaphores. Data moves between devices by JAX's collectives and lax.ppermute only.
A program may use at most 128 MiB of HBM per device.

v0:
```python
import functools

import jax
import jax.numpy as jnp
from jax import lax
from jax.experimental import pallas as pl
from jax.experimental.pallas import tpu as pltpu
from jax.sharding import PartitionSpec as P

SLICES = 4
STEPS = 2
INFO = 128
VMEM_LIMIT = 32 * 1024 * 1024


def from_behind(block, axis, distance):
    devices = range(lax.axis_size(axis))
    route = [(i - distance, i) for i in devices if i - distance in devices]
    return lax.ppermute(block, axis, route)


def swap_cores(block):
    devices = range(lax.axis_size("expert"))
    return lax.ppermute(block, "expert", [(i, i ^ 1) for i in devices])


def hop(block, outward, distance=1):
    devices = lax.axis_size("expert")
    chips = devices // 2
    route = []
    for i in range(devices):
        z, core = divmod(i, 2)
        way = 1 if core == 0 else -1
        target = (z + way * distance) % chips
        if distance == 2 and target // 2 != (z + way) % chips // 2:
            continue
        pair = (i, 2 * target + core)
        route.append(pair if outward else pair[::-1])
    return lax.ppermute(block, "expert", route)


def row_info(routes, gate_weights, first_slot):
    lanes, tokens, top = routes.shape
    experts = lax.axis_size("expert") // SLICES
    names = routes[..., None] == jnp.arange(experts, dtype=jnp.int32)
    chosen = jnp.sum(names.astype(jnp.int32), axis=2)
    rank = jnp.cumsum(chosen, axis=1) - chosen
    slots = jnp.sum(jnp.where(names, rank[:, :, None, :], 0), axis=-1) + first_slot
    info = jnp.concatenate(
        [routes.astype(jnp.bfloat16), gate_weights, slots.astype(jnp.bfloat16)], axis=-1
    )
    return jnp.pad(info, ((0, 0), (0, 0), (0, INFO - 3 * top)))


def sort_matrix(info, capacity, first, second):
    lanes, rows, _ = info.shape
    tokens = rows // 2
    ids = info[..., :2].astype(jnp.float32).reshape(lanes, 2, tokens, 2)
    key = jnp.where(
        jnp.any(ids == first, axis=-1), 0, jnp.where(jnp.any(ids == second, axis=-1), 1, 2)
    )
    order = key * tokens + jnp.arange(tokens)
    rank = jnp.sum((order[..., None, :] < order[..., :, None]).astype(jnp.int32), axis=-1)
    block = jnp.arange(2)[:, None]
    rest = tokens - 2 * capacity
    place = jnp.where(
        rank < capacity,
        block * capacity + rank,
        jnp.where(
            rank < 2 * capacity,
            2 * capacity + block * capacity + rank - capacity,
            4 * capacity + block * rest + rank - 2 * capacity,
        ),
    ).reshape(lanes, 1, rows)
    return (place == jnp.arange(rows)[:, None]).astype(jnp.bfloat16)


def expert_kernel(blocks, where_ref, *refs):
    xs, refs = refs[: 2 * blocks], refs[2 * blocks :]
    pres, (down_ref, up_ref), outs = refs[:blocks], refs[blocks : blocks + 2], refs[blocks + 2 :]
    width = outs[0].shape[1]
    chunk = 512 if width % 512 == 0 else 128
    expert = where_ref[0].astype(jnp.float32)
    slots = pres[0].shape[3]
    gates, placed = [], []
    for x_ref in xs:
        info = x_ref[:, width:].astype(jnp.float32)
        first = info[:, 0:1] == expert
        second = info[:, 1:2] == expert
        gates.append(jnp.where(first, info[:, 2:3], jnp.where(second, info[:, 3:4], 0.0)))
        slot = jnp.where(first, info[:, 4:5], jnp.where(second, info[:, 5:6], -1.0))
        column = lax.broadcasted_iota(jnp.int32, (x_ref.shape[0], slots), 1).astype(jnp.float32)
        placed.append(jnp.where(slot == column, 1.0, 0.0).astype(jnp.bfloat16))
    routed = []
    for start in range(0, width, chunk):
        routed.append(
            jnp.concatenate(
                [
                    x_ref[:, start : start + chunk].astype(jnp.float32) * gate
                    for x_ref, gate in zip(xs, gates)
                ],
                axis=0,
            ).astype(jnp.bfloat16)
        )
    across = (((1,), (1,)), ((), ()))
    preact = jnp.concatenate(
        [
            jnp.dot(placed[i], pres[i // 2][0, i % 2, 0], preferred_element_type=jnp.float32)
            for i in range(2 * blocks)
        ],
        axis=0,
    )
    logistic = jax.nn.sigmoid(preact)
    factor = logistic * (1.0 + preact * (1.0 - logistic))
    hidden = jnp.zeros(factor.shape, jnp.float32)
    for k, part in enumerate(routed):
        hidden = hidden + lax.dot_general(
            part,
            down_ref[:, k * chunk : (k + 1) * chunk],
            across,
            preferred_element_type=jnp.float32,
        )
    pre_grad = (hidden * factor).astype(jnp.bfloat16)
    for start in range(0, width, chunk):
        piece = lax.dot_general(
            pre_grad, up_ref[start : start + chunk, :], across, preferred_element_type=jnp.float32
        )
        row = 0
        for out_ref in outs:
            rows = out_ref.shape[0]
            out_ref[:, start : start + chunk] = piece[row : row + rows].astype(out_ref.dtype)
            row += rows


def expert_rows(step_now, expert, blocks, pre, down, up, wait_for=None):
    origins, lanes_of = zip(*blocks)
    xs = [x for lanes in lanes_of for x in lanes]
    hidden, width = down.shape
    _, lanes, _, slots, _ = pre.shape
    rows = sum(x.shape[0] for x in xs)
    once = pl.Buffered(1)
    scalars = jnp.stack([expert, *origins]).astype(jnp.int32)
    if wait_for is not None:
        scalars = lax.optimization_barrier((scalars, wait_for))[0]

    def pre_block(i):
        return pl.BlockSpec(
            (1, lanes, 1, slots, hidden), lambda g, s: (step_now, 0, s[1 + i], 0, 0)
        )

    def whole(shape):
        return pl.BlockSpec(shape, lambda g, s: (0,) * len(shape), pipeline_mode=once)

    outs = [jax.ShapeDtypeStruct((x.shape[0], width), jnp.bfloat16) for x in xs]
    sums = pl.pallas_call(
        functools.partial(expert_kernel, len(blocks)),
        out_shape=outs,
        grid_spec=pltpu.PrefetchScalarGridSpec(
            num_scalar_prefetch=1,
            grid=(1,),
            in_specs=[
                *[whole(x.shape) for x in xs],
                *[pre_block(i) for i in range(len(blocks))],
                whole(down.shape),
                whole(up.shape),
            ],
            out_specs=[whole(out.shape) for out in outs],
        ),
        compiler_params=pltpu.CompilerParams(vmem_limit_bytes=VMEM_LIMIT),
        cost_estimate=pl.CostEstimate(
            flops=4 * rows * hidden * width,
            bytes_accessed=4 * hidden * width + 4 * rows * width,
            transcendentals=rows * hidden,
        ),
    )(scalars, *xs, *[pre] * len(blocks), down, up)
    return [sums[2 * i : 2 * i + 2] for i in range(len(blocks))]


def add_rows(own, arrived):
    short = own.shape[0] - arrived.shape[0]
    arrived = jnp.pad(arrived.astype(jnp.float32), ((0, short), (0, 0)))
    return (own.astype(jnp.float32) + arrived).astype(jnp.bfloat16)


def body(grad_in, fresh_grad, routes, gate_weights, saved_pre, w_up, w_down):
    section_id = lax.axis_index("section")
    sections = lax.axis_size("section")
    groups = lax.axis_size("expert")
    device = lax.axis_index("expert")
    _, lanes, tokens, width = grad_in.shape
    chips, core = groups // 2, lax.rem(device, 2)
    chip, expert = lax.div(device, 2), lax.div(device, SLICES)
    experts = groups // SLICES
    capacity = saved_pre.shape[3] // groups
    half = chips // 2
    way = 1 - 2 * core
    outer = jnp.where(lax.rem(chip, 2) == 1 - core, 1, 0)
    first = lax.rem(experts + expert + way * (experts // 2 - 1 + outer), experts)
    second = lax.rem(experts + expert + way * (experts // 2 - 2 + outer), experts)
    sizes = [2 * tokens] * (half - 4) + [4 * capacity] * 2 + [2 * capacity] * 2

    pre = jnp.concatenate([saved_pre[0], swap_cores(saved_pre[0])], axis=-1)
    pre = pre.reshape(STEPS, lanes, chips, 2 * capacity, pre.shape[-1])
    down = jnp.concatenate([w_down[0], swap_cores(w_down[0])], axis=0)
    up = jnp.concatenate([w_up[0], swap_cores(w_up[0])], axis=1)
    current = grad_in[0]
    for step_now in range(STEPS):
        info = row_info(routes[0, step_now], gate_weights[0, step_now], core * capacity)
        mine = jnp.concatenate([current, info], axis=-1)
        both = jnp.concatenate([mine, swap_cores(mine)], axis=1)
        sorting = sort_matrix(both[..., width:], capacity, first, second)
        payload = jnp.einsum(
            "kpr,krd->kpd", sorting, both, preferred_element_type=jnp.float32
        ).astype(jnp.bfloat16)
        def compute(blocks, wait_for=None):
            return expert_rows(step_now, expert, blocks, pre, down, up, wait_for)

        streams = [payload[lane] for lane in range(lanes)]
        blocks = [(chip, mine)]
        for distance, size in enumerate(sizes, 1):
            far = distance == half
            arrived = [hop(s[:size], True, 2 if far else 1) for s in streams]
            blocks.append((lax.rem(chips + chip - way * distance, chips), arrived))
            if distance < half - 1:
                streams = arrived
        last = compute(blocks[half - 1 :])
        own, *late = compute([blocks[0], *blocks[half - 3 : half - 1]])
        sums = [
            add_rows(add_rows(o, hop(t, False)), hop(u, False, 2)) for o, t, u in zip(late[1], *last)
        ]
        partials = {half - 3: late[0]}
        for distance in range(half - 2, 0, -1):
            if distance - 1 not in partials and distance > 1:
                partials[distance - 2], partials[distance - 1] = compute(
                    blocks[distance - 2 : distance], sums[0]
                )
            sums = [hop(s, False) for s in sums]
            if distance > 1:
                sums = [add_rows(o, s) for o, s in zip(partials[distance - 1], sums)]
        arrived = jnp.einsum(
            "kpr,kpd->krd", sorting, jnp.stack(sums), preferred_element_type=jnp.float32
        ).astype(jnp.bfloat16)
        crossed = swap_cores(arrived[:, tokens:])
        result = (
            current.astype(jnp.float32)
            + jnp.stack(own).astype(jnp.float32)
            + arrived[:, :tokens].astype(jnp.float32)
            + crossed.astype(jnp.float32)
        ).astype(jnp.bfloat16)
        if step_now + 1 < STEPS:
            from_above = from_behind(result[0], "section", -1)
            from_below = from_behind(result[1], "section", 1)
            toward_lower = jnp.where(section_id == sections - 1, fresh_grad[0], from_above)
            toward_higher = jnp.where(section_id == 0, fresh_grad[1], from_below)
            current = jnp.stack([toward_lower, toward_higher])
    return result[None]


def solution(mesh):
    placed = (
        P("section", None, "expert", None),
        P(None, "expert", None),
        P("section", None, None, "expert", None),
        P("section", None, None, "expert", None),
        P("section", None, None, None, "expert"),
        P("section", None, "expert"),
        P("section", "expert", None),
    )
    return jax.shard_map(
        body,
        mesh=mesh,
        in_specs=placed,
        out_specs=P("section", None, "expert", None),
        check_vma=False,
    )
```

profile of v0, /device:TPU:25, one launch (start us, length us, event | category | flops | bytes accessed | tf_op | source)
XLA Modules:
  0.0 401.2 jit_solution(3951375612224409238)
XLA Ops:
  8.7 11.1 %collective-permute-start.1 = (bf16[64,3712]{1,0:T(8,128)(2,1)S(1)}, bf16[64,3712]{1,0:T(8,128)(2,1)S(1)}, u32[]{:S(2)}, u32[]{:S(2)}) collective-permute-start(bf16[64,3712]{1,0:T(8,128)(2,1)S(1)} %get-tuple-element.92), channel_id=1, source_target_pairs={{0,2},{1,31},{2,4},{3,1},{4,6},{5,3},{6,8},{7,5},{8,10},{9,7},{10,... | collective-permute-start | bytes 1425416 | tf_op jit(solution)/shard_map/ppermute | solution.py:39
  25.4 5.0 %collective-permute-start.2 = (bf16[64,3712]{1,0:T(8,128)(2,1)S(1)}, bf16[64,3712]{1,0:T(8,128)(2,1)S(1)}, u32[]{:S(2)}, u32[]{:S(2)}) collective-permute-start(bf16[64,3712]{1,0:T(8,128)(2,1)S(1)} %collective-permute-done.1.refs_0_), channel_id=1, source_target_pairs={{0,2},{1,31},{2,4},{3,1},{4,6},{5,3},{6,8},{7,5},{8,10},{9,7},{10,... | collective-permute-start | bytes 1425416 | tf_op jit(solution)/shard_map/ppermute | solution.py:39
  30.5 5.0 %collective-permute-start.7 = (bf16[64,3712]{1,0:T(8,128)(2,1)S(1)}, bf16[64,3712]{1,0:T(8,128)(2,1)S(1)}, u32[]{:S(2)}, u32[]{:S(2)}) collective-permute-start(bf16[64,3712]{1,0:T(8,128)(2,1)S(1)} %collective-permute-done.6.refs_1_), channel_id=1, source_target_pairs={{0,2},{1,31},{2,4},{3,1},{4,6},{5,3},{6,8},{7,5},{8,10},{9,7},{10,... | collective-permute-start | bytes 1425416 | tf_op jit(solution)/shard_map/ppermute | solution.py:39
  41.1 5.0 %collective-permute-start.8 = (bf16[64,3712]{1,0:T(8,128)(2,1)S(1)}, bf16[64,3712]{1,0:T(8,128)(2,1)S(1)}, u32[]{:S(2)}, u32[]{:S(2)}) collective-permute-start(bf16[64,3712]{1,0:T(8,128)(2,1)S(1)} %collective-permute-done.7.refs_3_), channel_id=1, source_target_pairs={{0,2},{1,31},{2,4},{3,1},{4,6},{5,3},{6,8},{7,5},{8,10},{9,7},{10,... | collective-permute-start | bytes 1425416 | tf_op jit(solution)/shard_map/ppermute | solution.py:39
  61.1 5.0 %collective-permute-start.5 = (bf16[48,3712]{1,0:T(8,128)(2,1)S(1)}, bf16[48,3712]{1,0:T(8,128)(2,1)S(1)}, u32[]{:S(2)}, u32[]{:S(2)}) collective-permute-start(bf16[48,3712]{1,0:T(8,128)(2,1)S(1)} %slice.113), channel_id=1, source_target_pairs={{0,2},{1,31},{2,4},{3,1},{4,6},{5,3},{6,8},{7,5},{8,10},{9,7},{10,... | collective-permute-start | bytes 1069064 | tf_op jit(solution)/shard_map/ppermute | solution.py:39
  66.2 5.0 %collective-permute-start.10 = (bf16[48,3712]{1,0:T(8,128)(2,1)S(1)}, bf16[48,3712]{1,0:T(8,128)(2,1)S(1)}, u32[]{:S(2)}, u32[]{:S(2)}) collective-permute-start(bf16[48,3712]{1,0:T(8,128)(2,1)S(1)} %slice.115), channel_id=1, source_target_pairs={{0,2},{1,31},{2,4},{3,1},{4,6},{5,3},{6,8},{7,5},{8,10},{9,7},{10,... | collective-permute-start | bytes 1069064 | tf_op jit(solution)/shard_map/ppermute | solution.py:39
  75.5 5.0 %collective-permute-start.12 = (bf16[48,3712]{1,0:T(8,128)(2,1)S(1)}, bf16[48,3712]{1,0:T(8,128)(2,1)S(1)}, u32[]{:S(2)}, u32[]{:S(2)}) collective-permute-start(bf16[48,3712]{1,0:T(8,128)(2,1)S(1)} %collective-permute-done.10.refs_3_), channel_id=1, source_target_pairs={{0,2},{1,31},{2,4},{3,1},{4,6},{5,3},{6,8},{7,5},{8,10},{9,7},{10,... | collective-permute-start | bytes 1069064 | tf_op jit(solution)/shard_map/ppermute | solution.py:39
  90.4 4.8 %collective-permute-start.19 = (bf16[24,3712]{1,0:T(8,128)(2,1)S(1)}, bf16[24,3712]{1,0:T(8,128)(2,1)S(1)}, u32[]{:S(2)}, u32[]{:S(2)}) collective-permute-start(bf16[24,3712]{1,0:T(8,128)(2,1)S(1)} %slice.117), channel_id=1, source_target_pairs={{1,29},{2,6},{5,1},{6,10},{9,5},{10,14},{13,9},{14,18},{17,13},{18... | collective-permute-start | bytes 534536 | tf_op jit(solution)/shard_map/ppermute | solution.py:39
  113.7 5.7 %collective-permute-start.30 = (bf16[48,3584]{1,0:T(8,128)(2,1)S(1)}, bf16[48,3584]{1,0:T(8,128)(2,1)S(1)}, u32[]{:S(2)}, u32[]{:S(2)}) collective-permute-start(bf16[48,3584]{1,0:T(8,128)(2,1)S(1)} %add_convert_fusion.25), channel_id=1, source_target_pairs={{2,0},{31,1},{4,2},{1,3},{6,4},{3,5},{8,6},{5,7},{10,8},{7,9},{12,... | collective-permute-start | bytes 1032200 | tf_op jit(solution)/shard_map/ppermute | solution.py:39
  176.9 5.1 %collective-permute-done.27 = bf16[64,3584]{1,0:T(8,128)(2,1)S(1)} collective-permute-done((bf16[64,3584]{1,0:T(8,128)(2,1)S(1)}, bf16[64,3584]{1,0:T(8,128)(2,1)S(1)}, u32[]{:S(2)}, u32[]{:S(2)}) %collective-permute-start.27) | collective-permute-done | bytes 458784 | tf_op jit(solution)/shard_map/ppermute | solution.py:39
  183.2 12.5 %collective-permute-start.36 = (bf16[2,32,3584]{2,1,0:T(8,128)(2,1)}, bf16[2,32,3584]{2,1,0:T(8,128)(2,1)}, u32[]{:S(2)}, u32[]{:S(2)}) collective-permute-start(bf16[2,32,3584]{2,1,0:T(8,128)(2,1)} %slice.119), channel_id=1, source_target_pairs={{0,1},{1,0},{2,3},{3,2},{4,5},{5,4},{6,7},{7,6},{8,9},{9,8},{10,11... | collective-permute-start | bytes 1376264 | tf_op jit(solution)/shard_map/ppermute | solution.py:24
  207.9 5.9 %collective-permute-done.38 = bf16[32,3584]{1,0:T(8,128)(2,1)S(1)} collective-permute-done((bf16[32,3584]{1,0:T(8,128)(2,1)S(1)}, bf16[32,3584]{1,0:T(8,128)(2,1)S(1)}, u32[]{:S(2)}, u32[]{:S(2)}) %collective-permute-start.38) | collective-permute-done | bytes 229408 | tf_op jit(solution)/shard_map/ppermute | solution.py:19
  220.0 5.6 %collective-permute-start.40 = (bf16[64,3712]{1,0:T(8,128)(2,1)S(1)}, bf16[64,3712]{1,0:T(8,128)(2,1)S(1)}, u32[]{:S(2)}, u32[]{:S(2)}) collective-permute-start(bf16[64,3712]{1,0:T(8,128)(2,1)S(1)} %get-tuple-element.90), channel_id=1, source_target_pairs={{0,2},{1,31},{2,4},{3,1},{4,6},{5,3},{6,8},{7,5},{8,10},{9,7},{10,... | collective-permute-start | bytes 1425416 | tf_op jit(solution)/shard_map/ppermute | solution.py:39
  231.1 5.0 %collective-permute-start.41 = (bf16[64,3712]{1,0:T(8,128)(2,1)S(1)}, bf16[64,3712]{1,0:T(8,128)(2,1)S(1)}, u32[]{:S(2)}, u32[]{:S(2)}) collective-permute-start(bf16[64,3712]{1,0:T(8,128)(2,1)S(1)} %collective-permute-done.40.refs_0_), channel_id=1, source_target_pairs={{0,2},{1,31},{2,4},{3,1},{4,6},{5,3},{6,8},{7,5},{8,10},{9,7},{10,... | collective-permute-start | bytes 1425416 | tf_op jit(solution)/shard_map/ppermute | solution.py:39
  236.2 5.0 %collective-permute-start.46 = (bf16[64,3712]{1,0:T(8,128)(2,1)S(1)}, bf16[64,3712]{1,0:T(8,128)(2,1)S(1)}, u32[]{:S(2)}, u32[]{:S(2)}) collective-permute-start(bf16[64,3712]{1,0:T(8,128)(2,1)S(1)} %collective-permute-done.45.refs_1_), channel_id=1, source_target_pairs={{0,2},{1,31},{2,4},{3,1},{4,6},{5,3},{6,8},{7,5},{8,10},{9,7},{10,... | collective-permute-start | bytes 1425416 | tf_op jit(solution)/shard_map/ppermute | solution.py:39
  241.7 5.0 %collective-permute-start.42 = (bf16[64,3712]{1,0:T(8,128)(2,1)S(1)}, bf16[64,3712]{1,0:T(8,128)(2,1)S(1)}, u32[]{:S(2)}, u32[]{:S(2)}) collective-permute-start(bf16[64,3712]{1,0:T(8,128)(2,1)S(1)} %collective-permute-done.41.refs_2_), channel_id=1, source_target_pairs={{0,2},{1,31},{2,4},{3,1},{4,6},{5,3},{6,8},{7,5},{8,10},{9,7},{10,... | collective-permute-start | bytes 1425416 | tf_op jit(solution)/shard_map/ppermute | solution.py:39
  246.8 5.0 %collective-permute-start.47 = (bf16[64,3712]{1,0:T(8,128)(2,1)S(1)}, bf16[64,3712]{1,0:T(8,128)(2,1)S(1)}, u32[]{:S(2)}, u32[]{:S(2)}) collective-permute-start(bf16[64,3712]{1,0:T(8,128)(2,1)S(1)} %collective-permute-done.46.refs_3_), channel_id=1, source_target_pairs={{0,2},{1,31},{2,4},{3,1},{4,6},{5,3},{6,8},{7,5},{8,10},{9,7},{10,... | collective-permute-start | bytes 1425416 | tf_op jit(solution)/shard_map/ppermute | solution.py:39
  252.3 5.0 %collective-permute-start.43 = (bf16[64,3712]{1,0:T(8,128)(2,1)S(1)}, bf16[64,3712]{1,0:T(8,128)(2,1)S(1)}, u32[]{:S(2)}, u32[]{:S(2)}) collective-permute-start(bf16[64,3712]{1,0:T(8,128)(2,1)S(1)} %collective-permute-done.42.refs_0_), channel_id=1, source_target_pairs={{0,2},{1,31},{2,4},{3,1},{4,6},{5,3},{6,8},{7,5},{8,10},{9,7},{10,... | collective-permute-start | bytes 1425416 | tf_op jit(solution)/shard_map/ppermute | solution.py:39
  257.4 5.0 %collective-permute-start.48 = (bf16[64,3712]{1,0:T(8,128)(2,1)S(1)}, bf16[64,3712]{1,0:T(8,128)(2,1)S(1)}, u32[]{:S(2)}, u32[]{:S(2)}) collective-permute-start(bf16[64,3712]{1,0:T(8,128)(2,1)S(1)} %collective-permute-done.47.refs_1_), channel_id=1, source_target_pairs={{0,2},{1,31},{2,4},{3,1},{4,6},{5,3},{6,8},{7,5},{8,10},{9,7},{10,... | collective-permute-start | bytes 1425416 | tf_op jit(solution)/shard_map/ppermute | solution.py:39
  263.0 5.0 %collective-permute-start.44 = (bf16[48,3712]{1,0:T(8,128)(2,1)S(1)}, bf16[48,3712]{1,0:T(8,128)(2,1)S(1)}, u32[]{:S(2)}, u32[]{:S(2)}) collective-permute-start(bf16[48,3712]{1,0:T(8,128)(2,1)S(1)} %slice.123), channel_id=1, source_target_pairs={{0,2},{1,31},{2,4},{3,1},{4,6},{5,3},{6,8},{7,5},{8,10},{9,7},{10,... | collective-permute-start | bytes 1069064 | tf_op jit(solution)/shard_map/ppermute | solution.py:39
  268.0 5.0 %collective-permute-start.49 = (bf16[48,3712]{1,0:T(8,128)(2,1)S(1)}, bf16[48,3712]{1,0:T(8,128)(2,1)S(1)}, u32[]{:S(2)}, u32[]{:S(2)}) collective-permute-start(bf16[48,3712]{1,0:T(8,128)(2,1)S(1)} %slice.125), channel_id=1, source_target_pairs={{0,2},{1,31},{2,4},{3,1},{4,6},{5,3},{6,8},{7,5},{8,10},{9,7},{10,... | collective-permute-start | bytes 1069064 | tf_op jit(solution)/shard_map/ppermute | solution.py:39
  277.4 5.0 %collective-permute-start.51 = (bf16[48,3712]{1,0:T(8,128)(2,1)S(1)}, bf16[48,3712]{1,0:T(8,128)(2,1)S(1)}, u32[]{:S(2)}, u32[]{:S(2)}) collective-permute-start(bf16[48,3712]{1,0:T(8,128)(2,1)S(1)} %collective-permute-done.49.refs_3_), channel_id=1, source_target_pairs={{0,2},{1,31},{2,4},{3,1},{4,6},{5,3},{6,8},{7,5},{8,10},{9,7},{10,... | collective-permute-start | bytes 1069064 | tf_op jit(solution)/shard_map/ppermute | solution.py:39
  378.6 4.9 %collective-permute-done.63 = bf16[64,3584]{1,0:T(8,128)(2,1)S(1)} collective-permute-done((bf16[64,3584]{1,0:T(8,128)(2,1)S(1)}, bf16[64,3584]{1,0:T(8,128)(2,1)S(1)}, u32[]{:S(2)}, u32[]{:S(2)}) %collective-permute-start.63) | collective-permute-done | bytes 458784 | tf_op jit(solution)/shard_map/ppermute | solution.py:39
  384.0 14.8 %collective-permute-start.72 = (bf16[2,32,3584]{2,1,0:T(8,128)(2,1)S(1)}, bf16[2,32,3584]{2,1,0:T(8,128)(2,1)S(1)}, u32[]{:S(2)}, u32[]{:S(2)}) collective-permute-start(bf16[2,32,3584]{2,1,0:T(8,128)(2,1)S(1)} %slice.129), channel_id=1, source_target_pairs={{0,1},{1,0},{2,3},{3,2},{4,5},{5,4},{6,7},{7,6},{8,9},{9,8},{10,11... | collective-permute-start | bytes 1376264 | tf_op jit(solution)/shard_map/ppermute | solution.py:24
  (269 shorter events, 254.3 us)
Async XLA Ops:
  8.7 16.7 %collective-permute-start.1 = (bf16[64,3712]{1,0:T(8,128)(2,1)S(1)}, bf16[64,3712]{1,0:T(8,128)(2,1)S(1)}, u32[]{:S(2)}, u32[]{:S(2)}) collective-permute-start(bf16[64,3712]{1,0:T(8,128)(2,1)S(1)} %get-tuple-element.92), channel_id=1, source_target_pairs={{0,2},{1,31},{2,4},{3,1},{4,6},{5,3},{6,8},{7,5},{8,10},{9,7},{10,... | collective-permute-start | bytes 1425416 | tf_op jit(solution)/shard_map/ppermute | solution.py:39
  19.8 10.7 %collective-permute-start.6 = (bf16[64,3712]{1,0:T(8,128)(2,1)S(1)}, bf16[64,3712]{1,0:T(8,128)(2,1)S(1)}, u32[]{:S(2)}, u32[]{:S(2)}) collective-permute-start(bf16[64,3712]{1,0:T(8,128)(2,1)S(1)} %get-tuple-element.91), channel_id=1, source_target_pairs={{0,2},{1,31},{2,4},{3,1},{4,6},{5,3},{6,8},{7,5},{8,10},{9,7},{10,... | collective-permute-start | bytes 1425416 | tf_op jit(solution)/shard_map/ppermute | solution.py:39
  25.4 12.0 %collective-permute-start.2 = (bf16[64,3712]{1,0:T(8,128)(2,1)S(1)}, bf16[64,3712]{1,0:T(8,128)(2,1)S(1)}, u32[]{:S(2)}, u32[]{:S(2)}) collective-permute-start(bf16[64,3712]{1,0:T(8,128)(2,1)S(1)} %collective-permute-done.1.refs_0_), channel_id=1, source_target_pairs={{0,2},{1,31},{2,4},{3,1},{4,6},{5,3},{6,8},{7,5},{8,10},{9,7},{10,... | collective-permute-start | bytes 1425416 | tf_op jit(solution)/shard_map/ppermute | solution.py:39
  35.5 45.0 %collective-permute-start.14 = (bf16[256,3584]{1,0:T(8,128)(2,1)}, bf16[256,3584]{1,0:T(8,128)(2,1)}, u32[]{:S(2)}, u32[]{:S(2)}) collective-permute-start(bf16[256,3584]{1,0:T(8,128)(2,1)} %bitcast.15), channel_id=1, source_target_pairs={{0,1},{1,0},{2,3},{3,2},{4,5},{5,4},{6,7},{7,6},{8,9},{9,8},{10,11... | collective-permute-start | bytes 5505032 | tf_op jit(solution)/shard_map/ppermute | solution.py:24
  37.4 13.9 %collective-permute-start.3 = (bf16[64,3712]{1,0:T(8,128)(2,1)S(1)}, bf16[64,3712]{1,0:T(8,128)(2,1)S(1)}, u32[]{:S(2)}, u32[]{:S(2)}) collective-permute-start(bf16[64,3712]{1,0:T(8,128)(2,1)S(1)} %collective-permute-done.2.refs_2_), channel_id=1, source_target_pairs={{0,2},{1,31},{2,4},{3,1},{4,6},{5,3},{6,8},{7,5},{8,10},{9,7},{10,... | collective-permute-start | bytes 1425416 | tf_op jit(solution)/shard_map/ppermute | solution.py:39
  41.1 14.4 %collective-permute-start.8 = (bf16[64,3712]{1,0:T(8,128)(2,1)S(1)}, bf16[64,3712]{1,0:T(8,128)(2,1)S(1)}, u32[]{:S(2)}, u32[]{:S(2)}) collective-permute-start(bf16[64,3712]{1,0:T(8,128)(2,1)S(1)} %collective-permute-done.7.refs_3_), channel_id=1, source_target_pairs={{0,2},{1,31},{2,4},{3,1},{4,6},{5,3},{6,8},{7,5},{8,10},{9,7},{10,... | collective-permute-start | bytes 1425416 | tf_op jit(solution)/shard_map/ppermute | solution.py:39
  46.9 48.2 %collective-permute-start.15 = (bf16[3584,256]{1,0:T(8,128)(2,1)}, bf16[3584,256]{1,0:T(8,128)(2,1)}, u32[]{:S(2)}, u32[]{:S(2)}) collective-permute-start(bf16[3584,256]{1,0:T(8,128)(2,1)} %bitcast.16), channel_id=1, source_target_pairs={{0,1},{1,0},{2,3},{3,2},{4,5},{5,4},{6,7},{7,6},{8,9},{9,8},{10,11... | collective-permute-start | bytes 5505032 | tf_op jit(solution)/shard_map/ppermute | solution.py:24
  48.8 22.5 %collective-permute-start.13 = (bf16[2,2,384,256]{3,2,1,0:T(8,128)(2,1)}, bf16[2,2,384,256]{3,2,1,0:T(8,128)(2,1)}, u32[]{:S(2)}, u32[]{:S(2)}) collective-permute-start(bf16[2,2,384,256]{3,2,1,0:T(8,128)(2,1)} %bitcast.13), channel_id=1, source_target_pairs={{0,1},{1,0},{2,3},{3,2},{4,5},{5,4},{6,7},{7,6},{8,9},{9,8},{10,11... | collective-permute-start | bytes 2359304 | tf_op jit(solution)/shard_map/ppermute | solution.py:24
  61.1 11.8 %collective-permute-start.5 = (bf16[48,3712]{1,0:T(8,128)(2,1)S(1)}, bf16[48,3712]{1,0:T(8,128)(2,1)S(1)}, u32[]{:S(2)}, u32[]{:S(2)}) collective-permute-start(bf16[48,3712]{1,0:T(8,128)(2,1)S(1)} %slice.113), channel_id=1, source_target_pairs={{0,2},{1,31},{2,4},{3,1},{4,6},{5,3},{6,8},{7,5},{8,10},{9,7},{10,... | collective-permute-start | bytes 1069064 | tf_op jit(solution)/shard_map/ppermute | solution.py:39
  75.5 12.9 %collective-permute-start.12 = (bf16[48,3712]{1,0:T(8,128)(2,1)S(1)}, bf16[48,3712]{1,0:T(8,128)(2,1)S(1)}, u32[]{:S(2)}, u32[]{:S(2)}) collective-permute-start(bf16[48,3712]{1,0:T(8,128)(2,1)S(1)} %collective-permute-done.10.refs_3_), channel_id=1, source_target_pairs={{0,2},{1,31},{2,4},{3,1},{4,6},{5,3},{6,8},{7,5},{8,10},{9,7},{10,... | collective-permute-start | bytes 1069064 | tf_op jit(solution)/shard_map/ppermute | solution.py:39
  82.8 14.6 %collective-permute-start.16 = (bf16[24,3712]{1,0:T(8,128)(2,1)S(1)}, bf16[24,3712]{1,0:T(8,128)(2,1)S(1)}, u32[]{:S(2)}, u32[]{:S(2)}) collective-permute-start(bf16[24,3712]{1,0:T(8,128)(2,1)S(1)} %slice.116), channel_id=1, source_target_pairs={{0,2},{1,31},{2,4},{3,1},{4,6},{5,3},{6,8},{7,5},{8,10},{9,7},{10,... | collective-permute-start | bytes 534536 | tf_op jit(solution)/shard_map/ppermute | solution.py:39
  84.8 12.7 %collective-permute-start.18 = (bf16[24,3712]{1,0:T(8,128)(2,1)S(1)}, bf16[24,3712]{1,0:T(8,128)(2,1)S(1)}, u32[]{:S(2)}, u32[]{:S(2)}) collective-permute-start(bf16[24,3712]{1,0:T(8,128)(2,1)S(1)} %slice.116), channel_id=1, source_target_pairs={{1,29},{2,6},{5,1},{6,10},{9,5},{10,14},{13,9},{14,18},{17,13},{18... | collective-permute-start | bytes 534536 | tf_op jit(solution)/shard_map/ppermute | solution.py:39
  100.8 12.8 %collective-permute-start.29 = (bf16[24,3584]{1,0:T(8,128)(2,1)S(1)}, bf16[24,3584]{1,0:T(8,128)(2,1)S(1)}, u32[]{:S(2)}, u32[]{:S(2)}) collective-permute-start(bf16[24,3584]{1,0:T(8,128)(2,1)S(1)} %get-tuple-element.64), channel_id=1, source_target_pairs={{29,1},{6,2},{1,5},{10,6},{5,9},{14,10},{9,13},{18,14},{13,17},{22... | collective-permute-start | bytes 516104 | tf_op jit(solution)/shard_map/ppermute | solution.py:39
  123.6 11.0 %collective-permute-start.31 = (bf16[48,3584]{1,0:T(8,128)(2,1)S(1)}, bf16[48,3584]{1,0:T(8,128)(2,1)S(1)}, u32[]{:S(2)}, u32[]{:S(2)}) collective-permute-start(bf16[48,3584]{1,0:T(8,128)(2,1)S(1)} %add_convert_fusion.24), channel_id=1, source_target_pairs={{2,0},{31,1},{4,2},{1,3},{6,4},{3,5},{8,6},{5,7},{10,8},{7,9},{12,... | collective-permute-start | bytes 1032200 | tf_op jit(solution)/shard_map/ppermute | solution.py:39
  138.5 11.6 %collective-permute-start.24 = (bf16[64,3584]{1,0:T(8,128)(2,1)S(1)}, bf16[64,3584]{1,0:T(8,128)(2,1)S(1)}, u32[]{:S(2)}, u32[]{:S(2)}) collective-permute-start(bf16[64,3584]{1,0:T(8,128)(2,1)S(1)} %add_convert_fusion.17), channel_id=1, source_target_pairs={{2,0},{31,1},{4,2},{1,3},{6,4},{3,5},{8,6},{5,7},{10,8},{7,9},{12,... | collective-permute-start | bytes 1376264 | tf_op jit(solution)/shard_map/ppermute | solution.py:39
  183.2 14.2 %collective-permute-start.36 = (bf16[2,32,3584]{2,1,0:T(8,128)(2,1)}, bf16[2,32,3584]{2,1,0:T(8,128)(2,1)}, u32[]{:S(2)}, u32[]{:S(2)}) collective-permute-start(bf16[2,32,3584]{2,1,0:T(8,128)(2,1)} %slice.119), channel_id=1, source_target_pairs={{0,1},{1,0},{2,3},{3,2},{4,5},{5,4},{6,7},{7,6},{8,9},{9,8},{10,11... | collective-permute-start | bytes 1376264 | tf_op jit(solution)/shard_map/ppermute | solution.py:24
  220.0 11.2 %collective-permute-start.40 = (bf16[64,3712]{1,0:T(8,128)(2,1)S(1)}, bf16[64,3712]{1,0:T(8,128)(2,1)S(1)}, u32[]{:S(2)}, u32[]{:S(2)}) collective-permute-start(bf16[64,3712]{1,0:T(8,128)(2,1)S(1)} %get-tuple-element.90), channel_id=1, source_target_pairs={{0,2},{1,31},{2,4},{3,1},{4,6},{5,3},{6,8},{7,5},{8,10},{9,7},{10,... | collective-permute-start | bytes 1425416 | tf_op jit(solution)/shard_map/ppermute | solution.py:39
  225.6 10.7 %collective-permute-start.45 = (bf16[64,3712]{1,0:T(8,128)(2,1)S(1)}, bf16[64,3712]{1,0:T(8,128)(2,1)S(1)}, u32[]{:S(2)}, u32[]{:S(2)}) collective-permute-start(bf16[64,3712]{1,0:T(8,128)(2,1)S(1)} %get-tuple-element.89), channel_id=1, source_target_pairs={{0,2},{1,31},{2,4},{3,1},{4,6},{5,3},{6,8},{7,5},{8,10},{9,7},{10,... | collective-permute-start | bytes 1425416 | tf_op jit(solution)/shard_map/ppermute | solution.py:39
  277.4 11.2 %collective-permute-start.51 = (bf16[48,3712]{1,0:T(8,128)(2,1)S(1)}, bf16[48,3712]{1,0:T(8,128)(2,1)S(1)}, u32[]{:S(2)}, u32[]{:S(2)}) collective-permute-start(bf16[48,3712]{1,0:T(8,128)(2,1)S(1)} %collective-permute-done.49.refs_3_), channel_id=1, source_target_pairs={{0,2},{1,31},{2,4},{3,1},{4,6},{5,3},{6,8},{7,5},{8,10},{9,7},{10,... | collective-permute-start | bytes 1069064 | tf_op jit(solution)/shard_map/ppermute | solution.py:39
  282.4 13.6 %collective-permute-start.52 = (bf16[24,3712]{1,0:T(8,128)(2,1)S(1)}, bf16[24,3712]{1,0:T(8,128)(2,1)S(1)}, u32[]{:S(2)}, u32[]{:S(2)}) collective-permute-start(bf16[24,3712]{1,0:T(8,128)(2,1)S(1)} %slice.126), channel_id=1, source_target_pairs={{0,2},{1,31},{2,4},{3,1},{4,6},{5,3},{6,8},{7,5},{8,10},{9,7},{10,... | collective-permute-start | bytes 534536 | tf_op jit(solution)/shard_map/ppermute | solution.py:39
  302.2 13.3 %collective-permute-start.65 = (bf16[24,3584]{1,0:T(8,128)(2,1)S(1)}, bf16[24,3584]{1,0:T(8,128)(2,1)S(1)}, u32[]{:S(2)}, u32[]{:S(2)}) collective-permute-start(bf16[24,3584]{1,0:T(8,128)(2,1)S(1)} %get-tuple-element.84), channel_id=1, source_target_pairs={{29,1},{6,2},{1,5},{10,6},{5,9},{14,10},{9,13},{18,14},{13,17},{22... | collective-permute-start | bytes 516104 | tf_op jit(solution)/shard_map/ppermute | solution.py:39
  325.5 10.9 %collective-permute-start.67 = (bf16[48,3584]{1,0:T(8,128)(2,1)S(1)}, bf16[48,3584]{1,0:T(8,128)(2,1)S(1)}, u32[]{:S(2)}, u32[]{:S(2)}) collective-permute-start(bf16[48,3584]{1,0:T(8,128)(2,1)S(1)} %add_convert_fusion.18), channel_id=1, source_target_pairs={{2,0},{31,1},{4,2},{1,3},{6,4},{3,5},{8,6},{5,7},{10,8},{7,9},{12,... | collective-permute-start | bytes 1032200 | tf_op jit(solution)/shard_map/ppermute | solution.py:39
  340.4 11.5 %collective-permute-start.60 = (bf16[64,3584]{1,0:T(8,128)(2,1)S(1)}, bf16[64,3584]{1,0:T(8,128)(2,1)S(1)}, u32[]{:S(2)}, u32[]{:S(2)}) collective-permute-start(bf16[64,3584]{1,0:T(8,128)(2,1)S(1)} %add_convert_fusion.8), channel_id=1, source_target_pairs={{2,0},{31,1},{4,2},{1,3},{6,4},{3,5},{8,6},{5,7},{10,8},{7,9},{12,... | collective-permute-start | bytes 1376264 | tf_op jit(solution)/shard_map/ppermute | solution.py:39
  384.0 16.3 %collective-permute-start.72 = (bf16[2,32,3584]{2,1,0:T(8,128)(2,1)S(1)}, bf16[2,32,3584]{2,1,0:T(8,128)(2,1)S(1)}, u32[]{:S(2)}, u32[]{:S(2)}) collective-permute-start(bf16[2,32,3584]{2,1,0:T(8,128)(2,1)S(1)} %slice.129), channel_id=1, source_target_pairs={{0,1},{1,0},{2,3},{3,2},{4,5},{5,4},{6,7},{7,6},{8,9},{9,8},{10,11... | collective-permute-start | bytes 1376264 | tf_op jit(solution)/shard_map/ppermute | solution.py:24
  (68 other events, 1027.3 us)
where the time goes:
time: 404 us; the launch traced here: 401 us
  starting transfers between devices  268 us (66%)
  waiting for transfers between devices  84.4 us (21%)
  Pallas kernels  25.7 us (6%)
  other arithmetic  15.1 us (4%)
  local copies, waits for them, and re-layouts  4.49 us (1%)
    ppermute x64, starting transfers between devices, hop(): return lax.ppermute(block, 'expert', route)  222 us
    ppermute x64, waiting for transfers between devices, hop(): return lax.ppermute(block, 'expert', route)  70.8 us
    ppermute x7, starting transfers between devices, swap_cores(): return lax.ppermute(block, 'expert', [(i, i ^ 1) for i in devices])  39.6 us
    pallas_call x8, Pallas kernels, expert_rows(): pl.pallas_call(functools.partial(expert_kernel, len(blocks)), out_shape=o...  25.7 us
    ppermute x2, waiting for transfers between devices, from_behind(): return lax.ppermute(block, axis, route)  8.46 us
  transfers between devices with their start and end apart: 73, of which 44 were waited for; matrix products, arithmetic and copies ran while one was open for 3% of the time, Pallas kernels for 5%

commit v1 on v0

--- a/solution.py
+++ b/solution.py
@@ -10,7 +10,7 @@
 SLICES = 4
 STEPS = 2
 INFO = 128
-VMEM_LIMIT = 32 * 1024 * 1024
+VMEM_LIMIT = 22 * 1024 * 1024
 
 
 def from_behind(block, axis, distance):
@@ -52,7 +52,7 @@
     return jnp.pad(info, ((0, 0), (0, 0), (0, INFO - 3 * top)))
 
 
-def sort_matrix(info, capacity, first, second):
+def sort_matrix(info, first, second):
     lanes, rows, _ = info.shape
     tokens = rows // 2
     ids = info[..., :2].astype(jnp.float32).reshape(lanes, 2, tokens, 2)
@@ -61,23 +61,14 @@
     )
     order = key * tokens + jnp.arange(tokens)
     rank = jnp.sum((order[..., None, :] < order[..., :, None]).astype(jnp.int32), axis=-1)
-    block = jnp.arange(2)[:, None]
-    rest = tokens - 2 * capacity
-    place = jnp.where(
-        rank < capacity,
-        block * capacity + rank,
-        jnp.where(
-            rank < 2 * capacity,
-            2 * capacity + block * capacity + rank - capacity,
-            4 * capacity + block * rest + rank - 2 * capacity,
-        ),
-    ).reshape(lanes, 1, rows)
+    place = (jnp.arange(2)[:, None] * tokens + rank).reshape(lanes, 1, rows)
     return (place == jnp.arange(rows)[:, None]).astype(jnp.bfloat16)
 
 
-def expert_kernel(blocks, where_ref, *refs):
-    xs, refs = refs[: 2 * blocks], refs[2 * blocks :]
-    pres, (down_ref, up_ref), outs = refs[:blocks], refs[blocks : blocks + 2], refs[blocks + 2 :]
+def expert_kernel(lane_of, origin_of, where_ref, *refs):
+    xs, refs = refs[: len(lane_of)], refs[len(lane_of) :]
+    outs, refs = refs[-len(lane_of) :], refs[: -len(lane_of)]
+    *pres, down_ref, up_ref = refs
     width = outs[0].shape[1]
     chunk = 512 if width % 512 == 0 else 128
     expert = where_ref[0].astype(jnp.float32)
@@ -91,34 +82,27 @@
         slot = jnp.where(first, info[:, 4:5], jnp.where(second, info[:, 5:6], -1.0))
         column = lax.broadcasted_iota(jnp.int32, (x_ref.shape[0], slots), 1).astype(jnp.float32)
         placed.append(jnp.where(slot == column, 1.0, 0.0).astype(jnp.bfloat16))
-    routed = []
-    for start in range(0, width, chunk):
-        routed.append(
-            jnp.concatenate(
-                [
-                    x_ref[:, start : start + chunk].astype(jnp.float32) * gate
-                    for x_ref, gate in zip(xs, gates)
-                ],
-                axis=0,
-            ).astype(jnp.bfloat16)
-        )
     across = (((1,), (1,)), ((), ()))
     preact = jnp.concatenate(
         [
-            jnp.dot(placed[i], pres[i // 2][0, i % 2, 0], preferred_element_type=jnp.float32)
-            for i in range(2 * blocks)
+            jnp.dot(rows, pres[origin][0, lane, 0], preferred_element_type=jnp.float32)
+            for rows, lane, origin in zip(placed, lane_of, origin_of)
         ],
         axis=0,
     )
     logistic = jax.nn.sigmoid(preact)
     factor = logistic * (1.0 + preact * (1.0 - logistic))
     hidden = jnp.zeros(factor.shape, jnp.float32)
-    for k, part in enumerate(routed):
+    for start in range(0, width, chunk):
+        routed = jnp.concatenate(
+            [
+                x_ref[:, start : start + chunk].astype(jnp.float32) * gate
+                for x_ref, gate in zip(xs, gates)
+            ],
+            axis=0,
+        ).astype(jnp.bfloat16)
         hidden = hidden + lax.dot_general(
-            part,
-            down_ref[:, k * chunk : (k + 1) * chunk],
-            across,
-            preferred_element_type=jnp.float32,
+            routed, down_ref[:, start : start + chunk], across, preferred_element_type=jnp.float32
         )
     pre_grad = (hidden * factor).astype(jnp.bfloat16)
     for start in range(0, width, chunk):
@@ -132,9 +116,11 @@
             row += rows
 
 
-def expert_rows(step_now, expert, blocks, pre, down, up, wait_for=None):
-    origins, lanes_of = zip(*blocks)
-    xs = [x for lanes in lanes_of for x in lanes]
+def expert_rows(step_now, expert, blocks, pre, down, up, wait_for=None, in_hbm=()):
+    origins = [origin for origin, _ in blocks]
+    xs = [x for _, streams in blocks for x in streams]
+    lane_of = [2 * i // len(streams) for _, streams in blocks for i in range(len(streams))]
+    origin_of = [k for k, (_, streams) in enumerate(blocks) for _ in streams]
     hidden, width = down.shape
     _, lanes, _, slots, _ = pre.shape
     rows = sum(x.shape[0] for x in xs)
@@ -142,6 +128,7 @@
     scalars = jnp.stack([expert, *origins]).astype(jnp.int32)
     if wait_for is not None:
         scalars = lax.optimization_barrier((scalars, wait_for))[0]
+        xs = [pltpu.with_memory_space_constraint(x, pltpu.HBM) for x in xs]
 
     def pre_block(i):
         return pl.BlockSpec(
@@ -151,9 +138,12 @@
     def whole(shape):
         return pl.BlockSpec(shape, lambda g, s: (0,) * len(shape), pipeline_mode=once)
 
-    outs = [jax.ShapeDtypeStruct((x.shape[0], width), jnp.bfloat16) for x in xs]
+    outs = [
+        (pltpu.HBM if owner in in_hbm else jax.ShapeDtypeStruct)((x.shape[0], width), jnp.bfloat16)
+        for x, owner in zip(xs, origin_of)
+    ]
     sums = pl.pallas_call(
-        functools.partial(expert_kernel, len(blocks)),
+        functools.partial(expert_kernel, lane_of, origin_of),
         out_shape=outs,
         grid_spec=pltpu.PrefetchScalarGridSpec(
             num_scalar_prefetch=1,
@@ -173,7 +163,9 @@
             transcendentals=rows * hidden,
         ),
     )(scalars, *xs, *[pre] * len(blocks), down, up)
-    return [sums[2 * i : 2 * i + 2] for i in range(len(blocks))]
+    return [
+        [s for s, owner in zip(sums, origin_of) if owner == k] for k in range(len(blocks))
+    ]
 
 
 def add_rows(own, arrived):
@@ -197,7 +189,7 @@
     outer = jnp.where(lax.rem(chip, 2) == 1 - core, 1, 0)
     first = lax.rem(experts + expert + way * (experts // 2 - 1 + outer), experts)
     second = lax.rem(experts + expert + way * (experts // 2 - 2 + outer), experts)
-    sizes = [2 * tokens] * (half - 4) + [4 * capacity] * 2 + [2 * capacity] * 2
+    sizes = [tokens] * (half - 4) + [2 * capacity] * 2
 
     pre = jnp.concatenate([saved_pre[0], swap_cores(saved_pre[0])], axis=-1)
     pre = pre.reshape(STEPS, lanes, chips, 2 * capacity, pre.shape[-1])
@@ -208,35 +200,43 @@
         info = row_info(routes[0, step_now], gate_weights[0, step_now], core * capacity)
         mine = jnp.concatenate([current, info], axis=-1)
         both = jnp.concatenate([mine, swap_cores(mine)], axis=1)
-        sorting = sort_matrix(both[..., width:], capacity, first, second)
+        sorting = sort_matrix(both[..., width:], first, second)
         payload = jnp.einsum(
             "kpr,krd->kpd", sorting, both, preferred_element_type=jnp.float32
         ).astype(jnp.bfloat16)
-        def compute(blocks, wait_for=None):
-            return expert_rows(step_now, expert, blocks, pre, down, up, wait_for)
-
-        streams = [payload[lane] for lane in range(lanes)]
+        def compute(blocks, *how):
+            return expert_rows(step_now, expert, blocks, pre, down, up, *how)
+
+        def compute(blocks, *how):
+            return expert_rows(step_now, expert, blocks, pre, down, up, *how)
+
+        def origin(distance):
+            return lax.rem(chips + chip - way * distance, chips)
+
+        streams = [payload[i // 2, i % 2 * tokens :][:tokens] for i in range(2 * lanes)]
         blocks = [(chip, mine)]
         for distance, size in enumerate(sizes, 1):
-            far = distance == half
-            arrived = [hop(s[:size], True, 2 if far else 1) for s in streams]
-            blocks.append((lax.rem(chips + chip - way * distance, chips), arrived))
-            if distance < half - 1:
-                streams = arrived
-        last = compute(blocks[half - 1 :])
-        own, *late = compute([blocks[0], *blocks[half - 3 : half - 1]])
-        sums = [
-            add_rows(add_rows(o, hop(t, False)), hop(u, False, 2)) for o, t, u in zip(late[1], *last)
+            streams = [hop(s[:size], True) for s in streams]
+            blocks.append((origin(distance), streams))
+        streams = [
+            jnp.concatenate([s[:capacity] for s in streams[2 * lane : 2 * lane + 2]], axis=0)
+            for lane in range(lanes)
         ]
-        partials = {half - 3: late[0]}
+        for distance in (1, 2):
+            arrived = [hop(s, True, distance) for s in streams]
+            blocks.append((origin(half - 2 + distance), arrived))
+        own, *partials, near, far = compute([blocks[0], *blocks[half - 3 :]], None, (0, 1, 2))
+        sums = [add_rows(hop(t, False), hop(u, False, 2)) for t, u in zip(near, far)]
+        sums = [s[b * capacity : (b + 1) * capacity] for s in sums for b in range(2)]
+        sums = [add_rows(o, s) for o, s in zip(partials[1], sums)]
+        partials = [None] * (half - 4) + partials
         for distance in range(half - 2, 0, -1):
-            if distance - 1 not in partials and distance > 1:
-                partials[distance - 2], partials[distance - 1] = compute(
-                    blocks[distance - 2 : distance], sums[0]
-                )
+            if distance == half - 3:
+                partials[: half - 4] = compute(blocks[1 : half - 3], sums[0])
             sums = [hop(s, False) for s in sums]
             if distance > 1:
-                sums = [add_rows(o, s) for o, s in zip(partials[distance - 1], sums)]
+                sums = [add_rows(o, s) for o, s in zip(partials[distance - 2], sums)]
+        sums = [jnp.concatenate(sums[2 * lane : 2 * lane + 2], axis=0) for lane in range(lanes)]
         arrived = jnp.einsum(
             "kpr,kpd->krd", sorting, jnp.stack(sums), preferred_element_type=jnp.float32
         ).astype(jnp.bfloat16)

time: 404 us -> 472 us (1.17)
  starting transfers between devices: 268 us -> 376 us
  waiting for transfers between devices: 84.4 us -> 36.4 us
  other arithmetic: 15.1 us -> 20 us
    ppermute x64 -> x112, starting transfers between devices: 222 us -> 320 us  [hop(): return lax.ppermute(block, 'expert', route)]
    ppermute x64 -> x112, waiting for transfers between devices: 70.8 us -> 22.6 us  [hop(): return lax.ppermute(block, 'expert', route)]
    ppermute x7, starting transfers between devices: 39.6 us -> 49.8 us  [swap_cores(): return lax.ppermute(block, 'expert', [(i, i ^ 1) for i in devices])]
    pallas_call x8 -> x4, Pallas kernels: 25.7 us -> 25.5 us  [expert_rows(): pl.pallas_call(functools.partial(expert_kernel, lane_of, origin_of), out_...]
  transfers between devices with their start and end apart: 73 -> 121, of which waited for: 44 -> 18; matrix products, arithmetic and copies ran while one was open for 3% -> 3% of each run, Pallas kernels for 5% -> 3%
where the time goes in v1:
time: 472 us; the launch traced here: 468 us
  starting transfers between devices  376 us (80%)
  waiting for transfers between devices  36.4 us (8%)
  Pallas kernels  25.5 us (5%)
  other arithmetic  20 us (4%)
  local copies, waits for them, and re-layouts  5.17 us (1%)
    ppermute x112, starting transfers between devices, hop(): return lax.ppermute(block, 'expert', route)  320 us
    ppermute x7, starting transfers between devices, swap_cores(): return lax.ppermute(block, 'expert', [(i, i ^ 1) for i in devices])  49.8 us
    pallas_call x4, Pallas kernels, expert_rows(): pl.pallas_call(functools.partial(expert_kernel, lane_of, origin_of), out_...  25.5 us
    ppermute x112, waiting for transfers between devices, hop(): return lax.ppermute(block, 'expert', route)  22.6 us
  transfers between devices with their start and end apart: 121, of which 18 were waited for; matrix products, arithmetic and copies ran while one was open for 3% of the time, Pallas kernels for 3%

profile of v1, /device:TPU:25, one launch (start us, length us, event | category | flops | bytes accessed | tf_op | source)
XLA Modules:
  0.0 468.0 jit_solution(7537754053915048403)
XLA Ops:
  8.7 11.1 %collective-permute-start.16 = (bf16[32,3712]{1,0:T(8,128)(2,1)S(1)}, bf16[32,3712]{1,0:T(8,128)(2,1)S(1)}, u32[]{:S(2)}, u32[]{:S(2)}) collective-permute-start(bf16[32,3712]{1,0:T(8,128)(2,1)S(1)} %get-tuple-element.145), channel_id=1, source_target_pairs={{0,2},{1,31},{2,4},{3,1},{4,6},{5,3},{6,8},{7,5},{8,10},{9,7},{10,... | collective-permute-start | bytes 712712 | tf_op jit(solution)/shard_map/ppermute | solution.py:39
  41.5 5.5 %collective-permute-start.29 = (bf16[2,2,384,256]{3,2,1,0:T(8,128)(2,1)S(1)}, bf16[2,2,384,256]{3,2,1,0:T(8,128)(2,1)S(1)}, u32[]{:S(2)}, u32[]{:S(2)}) collective-permute-start(bf16[2,2,384,256]{3,2,1,0:T(8,128)(2,1)S(1)} %bitcast.88), channel_id=1, source_target_pairs={{0,1},{1,0},{2,3},{3,2},{4,5},{5,4},{6,7},{7,6},{8,9},{9,8},{10,11... | collective-permute-start | bytes 2359304 | tf_op jit(solution)/shard_map/ppermute | solution.py:24
  64.1 4.6 collective-permute-start.31
  68.8 4.9 %collective-permute-start.20 = (bf16[24,3712]{1,0:T(8,128)(2,1)S(1)}, bf16[24,3712]{1,0:T(8,128)(2,1)S(1)}, u32[]{:S(2)}, u32[]{:S(2)}) collective-permute-start(bf16[24,3712]{1,0:T(8,128)(2,1)S(1)} %slice.211), channel_id=1, source_target_pairs={{0,2},{1,31},{2,4},{3,1},{4,6},{5,3},{6,8},{7,5},{8,10},{9,7},{10,... | collective-permute-start | bytes 534536 | tf_op jit(solution)/shard_map/ppermute | solution.py:39
  103.4 4.3 collective-permute-start.27
  115.6 5.3 %shard_map.73 = (bf16[32,3584]{1,0:T(8,128)(2,1)}, bf16[32,3584]{1,0:T(8,128)(2,1)}, bf16[24,3584]{1,0:T(8,128)(2,1)}, bf16[24,3584]{1,0:T(8,128)(2,1)}, bf16[24...) custom-call(s32[6]{0:T(128)S(1)} %stack.101.where_ref, ...), custom_call_target="tpu_custom_call" | custom-call | flops 2583691264 | bytes 12386304 | tf_op jit(solution)/shard_map/pallas_call | solution.py:145
  128.3 4.3 collective-permute-start.47
  157.2 4.8 %collective-permute-start.35 = (bf16[24,3584]{1,0:T(8,128)(2,1)S(1)}, bf16[24,3584]{1,0:T(8,128)(2,1)S(1)}, u32[]{:S(2)}, u32[]{:S(2)}) collective-permute-start(bf16[24,3584]{1,0:T(8,128)(2,1)S(1)} %add_convert_fusion.51), channel_id=1, source_target_pairs={{2,0},{31,1},{4,2},{1,3},{6,4},{3,5},{8,6},{5,7},{10,8},{7,9},{12,... | collective-permute-start | bytes 516104 | tf_op jit(solution)/shard_map/ppermute | solution.py:39
  164.0 7.5 %shard_map.74 = (bf16[32,3584]{1,0:T(8,128)(2,1)S(1)}, bf16[32,3584]{1,0:T(8,128)(2,1)S(1)}, bf16[32,3584]{1,0:T(8,128)(2,1)S(1)}, bf16[32,3584]{1,0:T(8,128)(2,...) custom-call(s32[5]{0:T(128)S(1)} %stack.109.where_ref, ...), custom_call_target="tpu_custom_call" | custom-call | flops 3758096384 | bytes 14680064 | tf_op jit(solution)/shard_map/pallas_call | solution.py:145
  179.5 4.8 %collective-permute-start.42 = (bf16[32,3584]{1,0:T(8,128)(2,1)S(1)}, bf16[32,3584]{1,0:T(8,128)(2,1)S(1)}, u32[]{:S(2)}, u32[]{:S(2)}) collective-permute-start(bf16[32,3584]{1,0:T(8,128)(2,1)S(1)} %add_convert_fusion.29), channel_id=1, source_target_pairs={{2,0},{31,1},{4,2},{1,3},{6,4},{3,5},{8,6},{5,7},{10,8},{7,9},{12,... | collective-permute-start | bytes 688136 | tf_op jit(solution)/shard_map/ppermute | solution.py:39
  212.9 4.6 collective-permute-start.45
  222.5 13.6 %collective-permute-start.60 = (bf16[2,32,3584]{2,1,0:T(8,128)(2,1)S(1)}, bf16[2,32,3584]{2,1,0:T(8,128)(2,1)}, u32[]{:S(2)}, u32[]{:S(2)}) collective-permute-start(bf16[2,32,3584]{2,1,0:T(8,128)(2,1)S(1)} %slice.219), channel_id=1, source_target_pairs={{0,1},{1,0},{2,3},{3,2},{4,5},{5,4},{6,7},{7,6},{8,9},{9,8},{10,11... | collective-permute-start | bytes 1376264 | tf_op jit(solution)/shard_map/ppermute | solution.py:24
  239.1 4.6 collective-permute-start.61
  248.2 5.9 %collective-permute-done.62 = bf16[32,3584]{1,0:T(8,128)(2,1)S(1)} collective-permute-done((bf16[32,3584]{1,0:T(8,128)(2,1)S(1)}, bf16[32,3584]{1,0:T(8,128)(2,1)S(1)}, u32[]{:S(2)}, u32[]{:S(2)}) %collective-permute-start.62) | collective-permute-done | bytes 229408 | tf_op jit(solution)/shard_map/ppermute | solution.py:19
  328.8 4.3 collective-permute-start.91
  344.5 5.2 %shard_map.75 = (bf16[32,3584]{1,0:T(8,128)(2,1)}, bf16[32,3584]{1,0:T(8,128)(2,1)}, bf16[24,3584]{1,0:T(8,128)(2,1)}, bf16[24,3584]{1,0:T(8,128)(2,1)}, bf16[24...) custom-call(s32[6]{0:T(128)S(1)} %stack.101.where_ref, ...), custom_call_target="tpu_custom_call" | custom-call | flops 2583691264 | bytes 12386304 | tf_op jit(solution)/shard_map/pallas_call | solution.py:145
  373.0 4.9 %collective-permute-start.108 = (bf16[24,3584]{1,0:T(8,128)(2,1)S(1)}, bf16[24,3584]{1,0:T(8,128)(2,1)S(1)}, u32[]{:S(2)}, u32[]{:S(2)}) collective-permute-start(bf16[24,3584]{1,0:T(8,128)(2,1)S(1)} %get-tuple-element.133), channel_id=1, source_target_pairs={{2,0},{31,1},{4,2},{1,3},{6,4},{3,5},{8,6},{5,7},{10,8},{7,9},{12,... | collective-permute-start | bytes 516104 | tf_op jit(solution)/shard_map/ppermute | solution.py:39
  384.6 4.6 collective-permute-start.109
  389.2 7.5 %shard_map.76 = (bf16[32,3584]{1,0:T(8,128)(2,1)S(1)}, bf16[32,3584]{1,0:T(8,128)(2,1)S(1)}, bf16[32,3584]{1,0:T(8,128)(2,1)S(1)}, bf16[32,3584]{1,0:T(8,128)(2,...) custom-call(s32[5]{0:T(128)S(1)} %stack.109.where_ref, ...), custom_call_target="tpu_custom_call" | custom-call | flops 3758096384 | bytes 14680064 | tf_op jit(solution)/shard_map/pallas_call | solution.py:145
  403.0 4.8 %collective-permute-start.102 = (bf16[32,3584]{1,0:T(8,128)(2,1)S(1)}, bf16[32,3584]{1,0:T(8,128)(2,1)S(1)}, u32[]{:S(2)}, u32[]{:S(2)}) collective-permute-start(bf16[32,3584]{1,0:T(8,128)(2,1)S(1)} %add_convert_fusion.13), channel_id=1, source_target_pairs={{2,0},{31,1},{4,2},{1,3},{6,4},{3,5},{8,6},{5,7},{10,8},{7,9},{12,... | collective-permute-start | bytes 688136 | tf_op jit(solution)/shard_map/ppermute | solution.py:39
  415.4 4.6 collective-permute-start.103
  426.5 4.9 %collective-permute-start.104 = (bf16[32,3584]{1,0:T(8,128)(2,1)S(1)}, bf16[32,3584]{1,0:T(8,128)(2,1)S(1)}, u32[]{:S(2)}, u32[]{:S(2)}) collective-permute-start(bf16[32,3584]{1,0:T(8,128)(2,1)S(1)} %add_convert_fusion.11), channel_id=1, source_target_pairs={{2,0},{31,1},{4,2},{1,3},{6,4},{3,5},{8,6},{5,7},{10,8},{7,9},{12,... | collective-permute-start | bytes 688136 | tf_op jit(solution)/shard_map/ppermute | solution.py:39
  438.1 4.6 collective-permute-start.105
  447.4 18.2 %collective-permute-start.120 = (bf16[2,32,3584]{2,1,0:T(8,128)(2,1)S(1)}, bf16[2,32,3584]{2,1,0:T(8,128)(2,1)S(1)}, u32[]{:S(2)}, u32[]{:S(2)}) collective-permute-start(bf16[2,32,3584]{2,1,0:T(8,128)(2,1)S(1)} %slice.237), channel_id=1, source_target_pairs={{0,1},{1,0},{2,3},{3,2},{4,5},{5,4},{6,7},{7,6},{8,9},{9,8},{10,11... | collective-permute-start | bytes 1376264 | tf_op jit(solution)/shard_map/ppermute | solution.py:24
  (469 shorter events, 315.5 us)
Async XLA Ops:
  8.7 19.1 %collective-permute-start.16 = (bf16[32,3712]{1,0:T(8,128)(2,1)S(1)}, bf16[32,3712]{1,0:T(8,128)(2,1)S(1)}, u32[]{:S(2)}, u32[]{:S(2)}) collective-permute-start(bf16[32,3712]{1,0:T(8,128)(2,1)S(1)} %get-tuple-element.145), channel_id=1, source_target_pairs={{0,2},{1,31},{2,4},{3,1},{4,6},{5,3},{6,8},{7,5},{8,10},{9,7},{10,... | collective-permute-start | bytes 712712 | tf_op jit(solution)/shard_map/ppermute | solution.py:39
  31.6 15.5 %collective-permute-start.12 = (bf16[32,3712]{1,0:T(8,128)(2,1)S(1)}, bf16[32,3712]{1,0:T(8,128)(2,1)S(1)}, u32[]{:S(2)}, u32[]{:S(2)}) collective-permute-start(bf16[32,3712]{1,0:T(8,128)(2,1)S(1)} %collective-permute-done.11.refs_2_), channel_id=1, source_target_pairs={{0,2},{1,31},{2,4},{3,1},{4,6},{5,3},{6,8},{7,5},{8,10},{9,7},{10,... | collective-permute-start | bytes 712712 | tf_op jit(solution)/shard_map/ppermute | solution.py:39
  34.3 16.7 %collective-permute-start.7 = (bf16[32,3712]{1,0:T(8,128)(2,1)S(1)}, bf16[32,3712]{1,0:T(8,128)(2,1)S(1)}, u32[]{:S(2)}, u32[]{:S(2)}) collective-permute-start(bf16[32,3712]{1,0:T(8,128)(2,1)S(1)} %collective-permute-done.6.refs_1_), channel_id=1, source_target_pairs={{0,2},{1,31},{2,4},{3,1},{4,6},{5,3},{6,8},{7,5},{8,10},{9,7},{10,... | collective-permute-start | bytes 712712 | tf_op jit(solution)/shard_map/ppermute | solution.py:39
  36.9 16.0 %collective-permute-start.2 = (bf16[32,3712]{1,0:T(8,128)(2,1)S(1)}, bf16[32,3712]{1,0:T(8,128)(2,1)S(1)}, u32[]{:S(2)}, u32[]{:S(2)}) collective-permute-start(bf16[32,3712]{1,0:T(8,128)(2,1)S(1)} %collective-permute-done.1.refs_0_), channel_id=1, source_target_pairs={{0,2},{1,31},{2,4},{3,1},{4,6},{5,3},{6,8},{7,5},{8,10},{9,7},{10,... | collective-permute-start | bytes 712712 | tf_op jit(solution)/shard_map/ppermute | solution.py:39
  39.6 15.3 %collective-permute-start.18 = (bf16[32,3712]{1,0:T(8,128)(2,1)S(1)}, bf16[32,3712]{1,0:T(8,128)(2,1)S(1)}, u32[]{:S(2)}, u32[]{:S(2)}) collective-permute-start(bf16[32,3712]{1,0:T(8,128)(2,1)S(1)} %collective-permute-done.17.refs_7_), channel_id=1, source_target_pairs={{0,2},{1,31},{2,4},{3,1},{4,6},{5,3},{6,8},{7,5},{8,10},{9,7},{10,... | collective-permute-start | bytes 712712 | tf_op jit(solution)/shard_map/ppermute | solution.py:39
  41.5 37.5 %collective-permute-start.29 = (bf16[2,2,384,256]{3,2,1,0:T(8,128)(2,1)S(1)}, bf16[2,2,384,256]{3,2,1,0:T(8,128)(2,1)S(1)}, u32[]{:S(2)}, u32[]{:S(2)}) collective-permute-start(bf16[2,2,384,256]{3,2,1,0:T(8,128)(2,1)S(1)} %bitcast.88), channel_id=1, source_target_pairs={{0,1},{1,0},{2,3},{3,2},{4,5},{5,4},{6,7},{7,6},{8,9},{9,8},{10,11... | collective-permute-start | bytes 2359304 | tf_op jit(solution)/shard_map/ppermute | solution.py:24
  59.0 14.7 %collective-permute-start.9 = (bf16[32,3712]{1,0:T(8,128)(2,1)S(1)}, bf16[32,3712]{1,0:T(8,128)(2,1)S(1)}, u32[]{:S(2)}, u32[]{:S(2)}) collective-permute-start(bf16[32,3712]{1,0:T(8,128)(2,1)S(1)} %collective-permute-done.8.refs_9_), channel_id=1, source_target_pairs={{0,2},{1,31},{2,4},{3,1},{4,6},{5,3},{6,8},{7,5},{8,10},{9,7},{10,... | collective-permute-start | bytes 712712 | tf_op jit(solution)/shard_map/ppermute | solution.py:39
  61.6 14.8 %collective-permute-start.4 = (bf16[32,3712]{1,0:T(8,128)(2,1)S(1)}, bf16[32,3712]{1,0:T(8,128)(2,1)S(1)}, u32[]{:S(2)}, u32[]{:S(2)}) collective-permute-start(bf16[32,3712]{1,0:T(8,128)(2,1)S(1)} %collective-permute-done.3.refs_8_), channel_id=1, source_target_pairs={{0,2},{1,31},{2,4},{3,1},{4,6},{5,3},{6,8},{7,5},{8,10},{9,7},{10,... | collective-permute-start | bytes 712712 | tf_op jit(solution)/shard_map/ppermute | solution.py:39
  64.1 43.5 %collective-permute-start.31 = (bf16[3584,256]{1,0:T(8,128)(2,1)}, bf16[3584,256]{1,0:T(8,128)(2,1)}, u32[]{:S(2)}, u32[]{:S(2)}) collective-permute-start(bf16[3584,256]{1,0:T(8,128)(2,1)} %bitcast.20), channel_id=1, source_target_pairs={{0,1},{1,0},{2,3},{3,2},{4,5},{5,4},{6,7},{7,6},{8,9},{9,8},{10,11... | collective-permute-start | bytes 5505032 | tf_op jit(solution)/shard_map/ppermute | solution.py:24
  79.1 32.9 %collective-permute-start.30 = (bf16[256,3584]{1,0:T(8,128)(2,1)}, bf16[256,3584]{1,0:T(8,128)(2,1)}, u32[]{:S(2)}, u32[]{:S(2)}) collective-permute-start(bf16[256,3584]{1,0:T(8,128)(2,1)} %bitcast.19), channel_id=1, source_target_pairs={{0,1},{1,0},{2,3},{3,2},{4,5},{5,4},{6,7},{7,6},{8,9},{9,8},{10,11... | collective-permute-start | bytes 5505032 | tf_op jit(solution)/shard_map/ppermute | solution.py:24
  98.3 17.3 %collective-permute-start.28 = (bf16[24,3712]{1,0:T(8,128)(2,1)S(1)}, bf16[24,3712]{1,0:T(8,128)(2,1)S(1)}, u32[]{:S(2)}, u32[]{:S(2)}) collective-permute-start(bf16[24,3712]{1,0:T(8,128)(2,1)S(1)} %pad_maximum_fusion.6), channel_id=1, source_target_pairs={{1,29},{2,6},{5,1},{6,10},{9,5},{10,14},{13,9},{14,18},{17,13},{18... | collective-permute-start | bytes 534536 | tf_op jit(solution)/shard_map/ppermute | solution.py:39
  101.4 14.2 %collective-permute-start.26 = (bf16[24,3712]{1,0:T(8,128)(2,1)S(1)}, bf16[24,3712]{1,0:T(8,128)(2,1)S(1)}, u32[]{:S(2)}, u32[]{:S(2)}) collective-permute-start(bf16[24,3712]{1,0:T(8,128)(2,1)S(1)} %pad_maximum_fusion.6), channel_id=1, source_target_pairs={{0,2},{1,31},{2,4},{3,1},{4,6},{5,3},{6,8},{7,5},{8,10},{9,7},{10,... | collective-permute-start | bytes 534536 | tf_op jit(solution)/shard_map/ppermute | solution.py:39
  150.0 29.4 %collective-permute-start.41 = (bf16[24,3584]{1,0:T(8,128)(2,1)S(1)}, bf16[24,3584]{1,0:T(8,128)(2,1)S(1)}, u32[]{:S(2)}, u32[]{:S(2)}) collective-permute-start(bf16[24,3584]{1,0:T(8,128)(2,1)S(1)} %add_convert_fusion.49), channel_id=1, source_target_pairs={{2,0},{31,1},{4,2},{1,3},{6,4},{3,5},{8,6},{5,7},{10,8},{7,9},{12,... | collective-permute-start | bytes 516104 | tf_op jit(solution)/shard_map/ppermute | solution.py:39
  152.9 20.6 %collective-permute-start.55 = (bf16[24,3584]{1,0:T(8,128)(2,1)S(1)}, bf16[24,3584]{1,0:T(8,128)(2,1)S(1)}, u32[]{:S(2)}, u32[]{:S(2)}) collective-permute-start(bf16[24,3584]{1,0:T(8,128)(2,1)S(1)} %add_convert_fusion.44), channel_id=1, source_target_pairs={{2,0},{31,1},{4,2},{1,3},{6,4},{3,5},{8,6},{5,7},{10,8},{7,9},{12,... | collective-permute-start | bytes 516104 | tf_op jit(solution)/shard_map/ppermute | solution.py:39
  155.2 22.3 %collective-permute-start.49 = (bf16[24,3584]{1,0:T(8,128)(2,1)S(1)}, bf16[24,3584]{1,0:T(8,128)(2,1)S(1)}, u32[]{:S(2)}, u32[]{:S(2)}) collective-permute-start(bf16[24,3584]{1,0:T(8,128)(2,1)S(1)} %add_convert_fusion.46), channel_id=1, source_target_pairs={{2,0},{31,1},{4,2},{1,3},{6,4},{3,5},{8,6},{5,7},{10,8},{7,9},{12,... | collective-permute-start | bytes 516104 | tf_op jit(solution)/shard_map/ppermute | solution.py:39
  157.2 14.3 %collective-permute-start.35 = (bf16[24,3584]{1,0:T(8,128)(2,1)S(1)}, bf16[24,3584]{1,0:T(8,128)(2,1)S(1)}, u32[]{:S(2)}, u32[]{:S(2)}) collective-permute-start(bf16[24,3584]{1,0:T(8,128)(2,1)S(1)} %add_convert_fusion.51), channel_id=1, source_target_pairs={{2,0},{31,1},{4,2},{1,3},{6,4},{3,5},{8,6},{5,7},{10,8},{7,9},{12,... | collective-permute-start | bytes 516104 | tf_op jit(solution)/shard_map/ppermute | solution.py:39
  222.5 15.1 %collective-permute-start.60 = (bf16[2,32,3584]{2,1,0:T(8,128)(2,1)S(1)}, bf16[2,32,3584]{2,1,0:T(8,128)(2,1)}, u32[]{:S(2)}, u32[]{:S(2)}) collective-permute-start(bf16[2,32,3584]{2,1,0:T(8,128)(2,1)S(1)} %slice.219), channel_id=1, source_target_pairs={{0,1},{1,0},{2,3},{3,2},{4,5},{5,4},{6,7},{7,6},{8,9},{9,8},{10,11... | collective-permute-start | bytes 1376264 | tf_op jit(solution)/shard_map/ppermute | solution.py:24
  366.7 13.2 %collective-permute-start.100 = (bf16[24,3584]{1,0:T(8,128)(2,1)S(1)}, bf16[24,3584]{1,0:T(8,128)(2,1)S(1)}, u32[]{:S(2)}, u32[]{:S(2)}) collective-permute-start(bf16[24,3584]{1,0:T(8,128)(2,1)S(1)} %add_convert_fusion.40), channel_id=1, source_target_pairs={{2,0},{31,1},{4,2},{1,3},{6,4},{3,5},{8,6},{5,7},{10,8},{7,9},{12,... | collective-permute-start | bytes 516104 | tf_op jit(solution)/shard_map/ppermute | solution.py:39
  378.0 18.7 %collective-permute-start.95 = (bf16[24,3584]{1,0:T(8,128)(2,1)S(1)}, bf16[24,3584]{1,0:T(8,128)(2,1)S(1)}, u32[]{:S(2)}, u32[]{:S(2)}) collective-permute-start(bf16[24,3584]{1,0:T(8,128)(2,1)S(1)} %add_convert_fusion.41), channel_id=1, source_target_pairs={{2,0},{31,1},{4,2},{1,3},{6,4},{3,5},{8,6},{5,7},{10,8},{7,9},{12,... | collective-permute-start | bytes 516104 | tf_op jit(solution)/shard_map/ppermute | solution.py:39
  380.0 22.9 %collective-permute-start.101 = (bf16[24,3584]{1,0:T(8,128)(2,1)S(1)}, bf16[24,3584]{1,0:T(8,128)(2,1)S(1)}, u32[]{:S(2)}, u32[]{:S(2)}) collective-permute-start(bf16[24,3584]{1,0:T(8,128)(2,1)S(1)} %add_convert_fusion.39), channel_id=1, source_target_pairs={{2,0},{31,1},{4,2},{1,3},{6,4},{3,5},{8,6},{5,7},{10,8},{7,9},{12,... | collective-permute-start | bytes 516104 | tf_op jit(solution)/shard_map/ppermute | solution.py:39
  382.6 16.1 %collective-permute-start.115 = (bf16[24,3584]{1,0:T(8,128)(2,1)S(1)}, bf16[24,3584]{1,0:T(8,128)(2,1)S(1)}, u32[]{:S(2)}, u32[]{:S(2)}) collective-permute-start(bf16[24,3584]{1,0:T(8,128)(2,1)S(1)} %add_convert_fusion.34), channel_id=1, source_target_pairs={{2,0},{31,1},{4,2},{1,3},{6,4},{3,5},{8,6},{5,7},{10,8},{7,9},{12,... | collective-permute-start | bytes 516104 | tf_op jit(solution)/shard_map/ppermute | solution.py:39
  384.6 16.1 %collective-permute-start.109 = (bf16[24,3584]{1,0:T(8,128)(2,1)S(1)}, bf16[24,3584]{1,0:T(8,128)(2,1)S(1)}, u32[]{:S(2)}, u32[]{:S(2)}) collective-permute-start(bf16[24,3584]{1,0:T(8,128)(2,1)S(1)} %add_convert_fusion.36), channel_id=1, source_target_pairs={{2,0},{31,1},{4,2},{1,3},{6,4},{3,5},{8,6},{5,7},{10,8},{7,9},{12,... | collective-permute-start | bytes 516104 | tf_op jit(solution)/shard_map/ppermute | solution.py:39
  431.5 12.9 %collective-permute-start.99 = (bf16[32,3584]{1,0:T(8,128)(2,1)S(1)}, bf16[32,3584]{1,0:T(8,128)(2,1)S(1)}, u32[]{:S(2)}, u32[]{:S(2)}) collective-permute-start(bf16[32,3584]{1,0:T(8,128)(2,1)S(1)} %add_convert_fusion.14), channel_id=1, source_target_pairs={{2,0},{31,1},{4,2},{1,3},{6,4},{3,5},{8,6},{5,7},{10,8},{7,9},{12,... | collective-permute-start | bytes 688136 | tf_op jit(solution)/shard_map/ppermute | solution.py:39
  447.4 19.6 %collective-permute-start.120 = (bf16[2,32,3584]{2,1,0:T(8,128)(2,1)S(1)}, bf16[2,32,3584]{2,1,0:T(8,128)(2,1)S(1)}, u32[]{:S(2)}, u32[]{:S(2)}) collective-permute-start(bf16[2,32,3584]{2,1,0:T(8,128)(2,1)S(1)} %slice.237), channel_id=1, source_target_pairs={{0,1},{1,0},{2,3},{3,2},{4,5},{5,4},{6,7},{7,6},{8,9},{9,8},{10,11... | collective-permute-start | bytes 1376264 | tf_op jit(solution)/shard_map/ppermute | solution.py:24
  (153 other events, 2729.3 us)

commit v2 on v0

--- a/solution.py
+++ b/solution.py
@@ -132,7 +132,7 @@
             row += rows
 
 
-def expert_rows(step_now, expert, blocks, pre, down, up, wait_for=None):
+def expert_rows(step_now, expert, blocks, pre, down, up, wait_for=None, in_hbm=True):
     origins, lanes_of = zip(*blocks)
     xs = [x for lanes in lanes_of for x in lanes]
     hidden, width = down.shape
@@ -151,7 +151,8 @@
     def whole(shape):
         return pl.BlockSpec(shape, lambda g, s: (0,) * len(shape), pipeline_mode=once)
 
-    outs = [jax.ShapeDtypeStruct((x.shape[0], width), jnp.bfloat16) for x in xs]
+    kind = pltpu.HBM if in_hbm else jax.ShapeDtypeStruct
+    outs = [kind((x.shape[0], width), jnp.bfloat16) for x in xs]
     sums = pl.pallas_call(
         functools.partial(expert_kernel, len(blocks)),
         out_shape=outs,
@@ -176,6 +177,10 @@
     return [sums[2 * i : 2 * i + 2] for i in range(len(blocks))]
 
 
+def after(blocks, sums):
+    return [lax.optimization_barrier((block, sums))[0] for block in blocks]
+
+
 def add_rows(own, arrived):
     short = own.shape[0] - arrived.shape[0]
     arrived = jnp.pad(arrived.astype(jnp.float32), ((0, short), (0, 0)))
@@ -212,31 +217,33 @@
         payload = jnp.einsum(
             "kpr,krd->kpd", sorting, both, preferred_element_type=jnp.float32
         ).astype(jnp.bfloat16)
-        def compute(blocks, wait_for=None):
-            return expert_rows(step_now, expert, blocks, pre, down, up, wait_for)
-
+        def compute(blocks, *how):
+            return expert_rows(step_now, expert, blocks, pre, down, up, *how)
+
+        ends = (half - 3, half - 2) if step_now == 0 else (half - 5, half - 3)
         streams = [payload[lane] for lane in range(lanes)]
-        blocks = [(chip, mine)]
+        blocks, partials = [], []
         for distance, size in enumerate(sizes, 1):
             far = distance == half
             arrived = [hop(s[:size], True, 2 if far else 1) for s in streams]
             blocks.append((lax.rem(chips + chip - way * distance, chips), arrived))
+            if distance in ends:
+                first_block = len(partials)
+                partials += compute(blocks[first_block : first_block + 2])
+                arrived = after(arrived, partials[-1][1])
             if distance < half - 1:
                 streams = arrived
-        last = compute(blocks[half - 1 :])
-        own, *late = compute([blocks[0], *blocks[half - 3 : half - 1]])
+        own, *late = compute([(chip, mine), *blocks[half - 4 : half - 2]])
+        partials += late
+        last = compute(blocks[half - 2 :], own[0], False)
         sums = [
-            add_rows(add_rows(o, hop(t, False)), hop(u, False, 2)) for o, t, u in zip(late[1], *last)
+            add_rows(add_rows(o, hop(t, False)), hop(u, False, 2))
+            for o, t, u in zip(partials[-1], *last)
         ]
-        partials = {half - 3: late[0]}
         for distance in range(half - 2, 0, -1):
-            if distance - 1 not in partials and distance > 1:
-                partials[distance - 2], partials[distance - 1] = compute(
-                    blocks[distance - 2 : distance], sums[0]
-                )
             sums = [hop(s, False) for s in sums]
             if distance > 1:
-                sums = [add_rows(o, s) for o, s in zip(partials[distance - 1], sums)]
+                sums = [add_rows(o, s) for o, s in zip(partials[distance - 2], sums)]
         arrived = jnp.einsum(
             "kpr,kpd->krd", sorting, jnp.stack(sums), preferred_element_type=jnp.float32
         ).astype(jnp.bfloat16)

time: 404 us -> 404 us (level)
  starting transfers between devices: 268 us -> 237 us
  waiting for transfers between devices: 84.4 us -> 109 us
  Pallas kernels: 25.7 us -> 33.1 us
    ppermute x64, starting transfers between devices: 222 us -> 193 us  [hop(): return lax.ppermute(block, 'expert', route)]
    ppermute x64, waiting for transfers between devices: 70.8 us -> 96.9 us  [hop(): return lax.ppermute(block, 'expert', route)]
    pallas_call x8, Pallas kernels: 25.7 us -> 33.1 us  [expert_rows(): pl.pallas_call(functools.partial(expert_kernel, len(blocks)), out_shape=o...]
  transfers between devices with their start and end apart: 73 -> 73, of which waited for: 44 -> 45; matrix products, arithmetic and copies ran while one was open for 3% -> 3% of each run, Pallas kernels for 5% -> 7%
where the time goes in v2:
time: 404 us; the launch traced here: 401 us
  starting transfers between devices  237 us (59%)
  waiting for transfers between devices  109 us (27%)
  Pallas kernels  33.1 us (8%)
  other arithmetic  13.6 us (3%)
  local copies, waits for them, and re-layouts  5.02 us (1%)
    ppermute x64, starting transfers between devices, hop(): return lax.ppermute(block, 'expert', route)  193 us
    ppermute x64, waiting for transfers between devices, hop(): return lax.ppermute(block, 'expert', route)  96.9 us
    ppermute x7, starting transfers between devices, swap_cores(): return lax.ppermute(block, 'expert', [(i, i ^ 1) for i in devices])  36.9 us
    pallas_call x8, Pallas kernels, expert_rows(): pl.pallas_call(functools.partial(expert_kernel, len(blocks)), out_shape=o...  33.1 us
    ppermute x2, waiting for transfers between devices, from_behind(): return lax.ppermute(block, axis, route)  8.46 us
  transfers between devices with their start and end apart: 73, of which 45 were waited for; matrix products, arithmetic and copies ran while one was open for 3% of the time, Pallas kernels for 7%

profile of v2, /device:TPU:25, one launch (start us, length us, event | category | flops | bytes accessed | tf_op | source)
XLA Modules:
  0.0 401.3 jit_solution(11230765617337088351)
XLA Ops:
  9.7 11.1 %collective-permute-start.1 = (bf16[64,3712]{1,0:T(8,128)(2,1)S(1)}, bf16[64,3712]{1,0:T(8,128)(2,1)S(1)}, u32[]{:S(2)}, u32[]{:S(2)}) collective-permute-start(bf16[64,3712]{1,0:T(8,128)(2,1)S(1)} %get-tuple-element.104), channel_id=1, source_target_pairs={{0,2},{1,31},{2,4},{3,1},{4,6},{5,3},{6,8},{7,5},{8,10},{9,7},{10,... | collective-permute-start | bytes 1425416 | tf_op jit(solution)/shard_map/ppermute | solution.py:39
  26.4 5.0 %collective-permute-start.2 = (bf16[64,3712]{1,0:T(8,128)(2,1)S(1)}, bf16[64,3712]{1,0:T(8,128)(2,1)S(1)}, u32[]{:S(2)}, u32[]{:S(2)}) collective-permute-start(bf16[64,3712]{1,0:T(8,128)(2,1)S(1)} %collective-permute-done.1.refs_0_), channel_id=1, source_target_pairs={{0,2},{1,31},{2,4},{3,1},{4,6},{5,3},{6,8},{7,5},{8,10},{9,7},{10,... | collective-permute-start | bytes 1425416 | tf_op jit(solution)/shard_map/ppermute | solution.py:39
  31.5 5.0 %collective-permute-start.7 = (bf16[64,3712]{1,0:T(8,128)(2,1)S(1)}, bf16[64,3712]{1,0:T(8,128)(2,1)S(1)}, u32[]{:S(2)}, u32[]{:S(2)}) collective-permute-start(bf16[64,3712]{1,0:T(8,128)(2,1)S(1)} %collective-permute-done.6.refs_1_), channel_id=1, source_target_pairs={{0,2},{1,31},{2,4},{3,1},{4,6},{5,3},{6,8},{7,5},{8,10},{9,7},{10,... | collective-permute-start | bytes 1425416 | tf_op jit(solution)/shard_map/ppermute | solution.py:39
  42.3 4.8 %collective-permute-start.8 = (bf16[64,3712]{1,0:T(8,128)(2,1)S(1)}, bf16[64,3712]{1,0:T(8,128)(2,1)S(1)}, u32[]{:S(2)}, u32[]{:S(2)}) collective-permute-start(bf16[64,3712]{1,0:T(8,128)(2,1)S(1)} %collective-permute-done.7.refs_3_), channel_id=1, source_target_pairs={{0,2},{1,31},{2,4},{3,1},{4,6},{5,3},{6,8},{7,5},{8,10},{9,7},{10,... | collective-permute-start | bytes 1425416 | tf_op jit(solution)/shard_map/ppermute | solution.py:39
  53.5 4.5 %collective-permute-start.9 = (bf16[64,3712]{1,0:T(8,128)(2,1)S(1)}, bf16[64,3712]{1,0:T(8,128)(2,1)S(1)}, u32[]{:S(2)}, u32[]{:S(2)}) collective-permute-start(bf16[64,3712]{1,0:T(8,128)(2,1)S(1)} %collective-permute-done.8.refs_1_), channel_id=1, source_target_pairs={{0,2},{1,31},{2,4},{3,1},{4,6},{5,3},{6,8},{7,5},{8,10},{9,7},{10,... | collective-permute-start | bytes 1425416 | tf_op jit(solution)/shard_map/ppermute | solution.py:39
  63.7 4.9 %collective-permute-start.10 = (bf16[48,3712]{1,0:T(8,128)(2,1)S(1)}, bf16[48,3712]{1,0:T(8,128)(2,1)S(1)}, u32[]{:S(2)}, u32[]{:S(2)}) collective-permute-start(bf16[48,3712]{1,0:T(8,128)(2,1)S(1)} %slice.115), channel_id=1, source_target_pairs={{0,2},{1,31},{2,4},{3,1},{4,6},{5,3},{6,8},{7,5},{8,10},{9,7},{10,... | collective-permute-start | bytes 1069064 | tf_op jit(solution)/shard_map/ppermute | solution.py:39
  71.0 4.5 %shard_map.73 = (bf16[64,3584]{1,0:T(8,128)(2,1)}, bf16[64,3584]{1,0:T(8,128)(2,1)}, bf16[64,3584]{1,0:T(8,128)(2,1)}, bf16[64,3584]{1,0:T(8,128)(2,1)}) custom-call(s32[3]{0:T(128)S(1)} %pad_add_fusion.1.where_ref, bf16[64,3712]{1,0:T(8,128)(2,1)S(1)} %collective-permute-done.1.refs_0_, bf16[64,3712]{1,0:T(8,128)(2,1)S(1)} %collective-permute-done.6.refs_1_, ...), custom_call_target="tpu_custom_call" | custom-call | flops 1879048192 | bytes 11010048 | tf_op jit(solution)/shard_map/pallas_call | solution.py:156
  87.7 4.8 %collective-permute-start.18 = (bf16[24,3712]{1,0:T(8,128)(2,1)S(1)}, bf16[24,3712]{1,0:T(8,128)(2,1)S(1)}, u32[]{:S(2)}, u32[]{:S(2)}) collective-permute-start(bf16[24,3712]{1,0:T(8,128)(2,1)S(1)} %slice.94), channel_id=1, source_target_pairs={{1,29},{2,6},{5,1},{6,10},{9,5},{10,14},{13,9},{14,18},{17,13},{18... | collective-permute-start | bytes 534536 | tf_op jit(solution)/shard_map/ppermute | solution.py:39
  97.1 4.5 %shard_map.74 = (bf16[32,3584]{1,0:T(8,128)(2,1)}, bf16[32,3584]{1,0:T(8,128)(2,1)}, bf16[48,3584]{1,0:T(8,128)(2,1)}, bf16[48,3584]{1,0:T(8,128)(2,1)}, bf16[48...) custom-call(s32[4]{0:T(128)S(1)} %pad_add_fusion.where_ref, bf16[32,3712]{1,0:T(8,128)(2,1)S(1)} %get-tuple-element.108.refs_0_, ...), custom_call_target="tpu_custom_call" | custom-call | flops 1879048192 | bytes 11010048 | tf_op jit(solution)/shard_map/pallas_call | solution.py:156
  177.2 5.1 %collective-permute-done.27 = bf16[64,3584]{1,0:T(8,128)(2,1)S(1)} collective-permute-done((bf16[64,3584]{1,0:T(8,128)(2,1)S(1)}, bf16[64,3584]{1,0:T(8,128)(2,1)S(1)}, u32[]{:S(2)}, u32[]{:S(2)}) %collective-permute-start.27) | collective-permute-done | bytes 458784 | tf_op jit(solution)/shard_map/ppermute | solution.py:39
  182.8 12.7 %collective-permute-start.36 = (bf16[2,32,3584]{2,1,0:T(8,128)(2,1)S(1)}, bf16[2,32,3584]{2,1,0:T(8,128)(2,1)}, u32[]{:S(2)}, u32[]{:S(2)}) collective-permute-start(bf16[2,32,3584]{2,1,0:T(8,128)(2,1)S(1)} %slice.117), channel_id=1, source_target_pairs={{0,1},{1,0},{2,3},{3,2},{4,5},{5,4},{6,7},{7,6},{8,9},{9,8},{10,11... | collective-permute-start | bytes 1376264 | tf_op jit(solution)/shard_map/ppermute | solution.py:24
  198.5 4.6 %collective-permute-start.37 = (bf16[32,3584]{1,0:T(8,128)(2,1)S(1)}, bf16[32,3584]{1,0:T(8,128)(2,1)S(1)}, u32[]{:S(2)}, u32[]{:S(2)}) collective-permute-start(bf16[32,3584]{1,0:T(8,128)(2,1)S(1)} %get-tuple-element.111), channel_id=1, source_target_pairs={{32,0},{64,32},{96,64},{128,96},{160,128},{192,160},{224,192},{256... | collective-permute-start | bytes 688136 | tf_op jit(solution)/shard_map/ppermute | solution.py:19
  207.7 5.9 %collective-permute-done.38 = bf16[32,3584]{1,0:T(8,128)(2,1)S(1)} collective-permute-done((bf16[32,3584]{1,0:T(8,128)(2,1)S(1)}, bf16[32,3584]{1,0:T(8,128)(2,1)S(1)}, u32[]{:S(2)}, u32[]{:S(2)}) %collective-permute-start.38) | collective-permute-done | bytes 229408 | tf_op jit(solution)/shard_map/ppermute | solution.py:19
  219.7 5.5 %collective-permute-start.40 = (bf16[64,3712]{1,0:T(8,128)(2,1)S(1)}, bf16[64,3712]{1,0:T(8,128)(2,1)S(1)}, u32[]{:S(2)}, u32[]{:S(2)}) collective-permute-start(bf16[64,3712]{1,0:T(8,128)(2,1)S(1)} %get-tuple-element.102), channel_id=1, source_target_pairs={{0,2},{1,31},{2,4},{3,1},{4,6},{5,3},{6,8},{7,5},{8,10},{9,7},{10,... | collective-permute-start | bytes 1425416 | tf_op jit(solution)/shard_map/ppermute | solution.py:39
  230.8 5.0 %collective-permute-start.41 = (bf16[64,3712]{1,0:T(8,128)(2,1)S(1)}, bf16[64,3712]{1,0:T(8,128)(2,1)S(1)}, u32[]{:S(2)}, u32[]{:S(2)}) collective-permute-start(bf16[64,3712]{1,0:T(8,128)(2,1)S(1)} %collective-permute-done.40.refs_0_), channel_id=1, source_target_pairs={{0,2},{1,31},{2,4},{3,1},{4,6},{5,3},{6,8},{7,5},{8,10},{9,7},{10,... | collective-permute-start | bytes 1425416 | tf_op jit(solution)/shard_map/ppermute | solution.py:39
  235.9 5.0 %collective-permute-start.44 = (bf16[64,3712]{1,0:T(8,128)(2,1)S(1)}, bf16[64,3712]{1,0:T(8,128)(2,1)S(1)}, u32[]{:S(2)}, u32[]{:S(2)}) collective-permute-start(bf16[64,3712]{1,0:T(8,128)(2,1)S(1)} %collective-permute-done.43.refs_1_), channel_id=1, source_target_pairs={{0,2},{1,31},{2,4},{3,1},{4,6},{5,3},{6,8},{7,5},{8,10},{9,7},{10,... | collective-permute-start | bytes 1425416 | tf_op jit(solution)/shard_map/ppermute | solution.py:39
  241.4 5.0 %collective-permute-start.42 = (bf16[64,3712]{1,0:T(8,128)(2,1)S(1)}, bf16[64,3712]{1,0:T(8,128)(2,1)S(1)}, u32[]{:S(2)}, u32[]{:S(2)}) collective-permute-start(bf16[64,3712]{1,0:T(8,128)(2,1)S(1)} %collective-permute-done.41.refs_2_), channel_id=1, source_target_pairs={{0,2},{1,31},{2,4},{3,1},{4,6},{5,3},{6,8},{7,5},{8,10},{9,7},{10,... | collective-permute-start | bytes 1425416 | tf_op jit(solution)/shard_map/ppermute | solution.py:39
  246.5 5.0 %collective-permute-start.47 = (bf16[64,3712]{1,0:T(8,128)(2,1)S(1)}, bf16[64,3712]{1,0:T(8,128)(2,1)S(1)}, u32[]{:S(2)}, u32[]{:S(2)}) collective-permute-start(bf16[64,3712]{1,0:T(8,128)(2,1)S(1)} %collective-permute-done.44.refs_3_), channel_id=1, source_target_pairs={{0,2},{1,31},{2,4},{3,1},{4,6},{5,3},{6,8},{7,5},{8,10},{9,7},{10,... | collective-permute-start | bytes 1425416 | tf_op jit(solution)/shard_map/ppermute | solution.py:39
  253.5 4.4 %shard_map.77 = (bf16[64,3584]{1,0:T(8,128)(2,1)}, bf16[64,3584]{1,0:T(8,128)(2,1)}, bf16[64,3584]{1,0:T(8,128)(2,1)}, bf16[64,3584]{1,0:T(8,128)(2,1)}) custom-call(s32[3]{0:T(128)S(1)} %pad_add_fusion.1.where_ref, bf16[64,3712]{1,0:T(8,128)(2,1)S(1)} %collective-permute-done.40.refs_0_, bf16[64,3712]{1,0:T(8,128)(2,1)S(1)} %collective-permute-done.43.refs_1_, ...), custom_call_target="tpu_custom_call" | custom-call | flops 1879048192 | bytes 11010048 | tf_op jit(solution)/shard_map/pallas_call | solution.py:156
  262.1 5.6 %collective-permute-done.45.refs_2_ = bf16[64,3712]{1,0:T(8,128)(2,1)S(1)} collective-permute-done((bf16[64,3712]{1,0:T(8,128)(2,1)S(1)}, bf16[64,3712]{1,0:T(8,128)(2,1)S(1)}, u32[]{:S(2)}, u32[]{:S(2)}) %collective-permute-start.45) | collective-permute-done | bytes 475168 | tf_op jit(solution)/shard_map/ppermute | solution.py:39
  291.3 4.8 %collective-permute-start.54 = (bf16[24,3712]{1,0:T(8,128)(2,1)S(1)}, bf16[24,3712]{1,0:T(8,128)(2,1)S(1)}, u32[]{:S(2)}, u32[]{:S(2)}) collective-permute-start(bf16[24,3712]{1,0:T(8,128)(2,1)S(1)} %slice.124), channel_id=1, source_target_pairs={{1,29},{2,6},{5,1},{6,10},{9,5},{10,14},{13,9},{14,18},{17,13},{18... | collective-permute-start | bytes 534536 | tf_op jit(solution)/shard_map/ppermute | solution.py:39
  301.8 4.4 %shard_map.79 = (bf16[32,3584]{1,0:T(8,128)(2,1)}, bf16[32,3584]{1,0:T(8,128)(2,1)}, bf16[48,3584]{1,0:T(8,128)(2,1)}, bf16[48,3584]{1,0:T(8,128)(2,1)}, bf16[48...) custom-call(s32[4]{0:T(128)S(1)} %pad_add_fusion.where_ref, bf16[32,3712]{1,0:T(8,128)(2,1)S(1)} %get-tuple-element.106.refs_0_, ...), custom_call_target="tpu_custom_call" | custom-call | flops 1879048192 | bytes 11010048 | tf_op jit(solution)/shard_map/pallas_call | solution.py:156
  380.9 5.1 %collective-permute-done.63 = bf16[64,3584]{1,0:T(8,128)(2,1)S(1)} collective-permute-done((bf16[64,3584]{1,0:T(8,128)(2,1)S(1)}, bf16[64,3584]{1,0:T(8,128)(2,1)S(1)}, u32[]{:S(2)}, u32[]{:S(2)}) %collective-permute-start.63) | collective-permute-done | bytes 458784 | tf_op jit(solution)/shard_map/ppermute | solution.py:39
  386.5 12.4 %collective-permute-start.72 = (bf16[2,32,3584]{2,1,0:T(8,128)(2,1)S(1)}, bf16[2,32,3584]{2,1,0:T(8,128)(2,1)S(1)}, u32[]{:S(2)}, u32[]{:S(2)}) collective-permute-start(bf16[2,32,3584]{2,1,0:T(8,128)(2,1)S(1)} %slice.127), channel_id=1, source_target_pairs={{0,1},{1,0},{2,3},{3,2},{4,5},{5,4},{6,7},{7,6},{8,9},{9,8},{10,11... | collective-permute-start | bytes 1376264 | tf_op jit(solution)/shard_map/ppermute | solution.py:24
  (303 shorter events, 260.5 us)
Async XLA Ops:
  6.0 52.0 %collective-permute-start.12 = (bf16[256,3584]{1,0:T(8,128)(2,1)}, bf16[256,3584]{1,0:T(8,128)(2,1)}, u32[]{:S(2)}, u32[]{:S(2)}) collective-permute-start(bf16[256,3584]{1,0:T(8,128)(2,1)} %bitcast.75), channel_id=1, source_target_pairs={{0,1},{1,0},{2,3},{3,2},{4,5},{5,4},{6,7},{7,6},{8,9},{9,8},{10,11... | collective-permute-start | bytes 5505032 | tf_op jit(solution)/shard_map/ppermute | solution.py:24
  9.7 16.7 %collective-permute-start.1 = (bf16[64,3712]{1,0:T(8,128)(2,1)S(1)}, bf16[64,3712]{1,0:T(8,128)(2,1)S(1)}, u32[]{:S(2)}, u32[]{:S(2)}) collective-permute-start(bf16[64,3712]{1,0:T(8,128)(2,1)S(1)} %get-tuple-element.104), channel_id=1, source_target_pairs={{0,2},{1,31},{2,4},{3,1},{4,6},{5,3},{6,8},{7,5},{8,10},{9,7},{10,... | collective-permute-start | bytes 1425416 | tf_op jit(solution)/shard_map/ppermute | solution.py:39
  23.5 45.2 %collective-permute-start.13 = (bf16[3584,256]{1,0:T(8,128)(2,1)}, bf16[3584,256]{1,0:T(8,128)(2,1)}, u32[]{:S(2)}, u32[]{:S(2)}) collective-permute-start(bf16[3584,256]{1,0:T(8,128)(2,1)} %bitcast.18), channel_id=1, source_target_pairs={{0,1},{1,0},{2,3},{3,2},{4,5},{5,4},{6,7},{7,6},{8,9},{9,8},{10,11... | collective-permute-start | bytes 5505032 | tf_op jit(solution)/shard_map/ppermute | solution.py:24
  26.4 12.2 %collective-permute-start.2 = (bf16[64,3712]{1,0:T(8,128)(2,1)S(1)}, bf16[64,3712]{1,0:T(8,128)(2,1)S(1)}, u32[]{:S(2)}, u32[]{:S(2)}) collective-permute-start(bf16[64,3712]{1,0:T(8,128)(2,1)S(1)} %collective-permute-done.1.refs_0_), channel_id=1, source_target_pairs={{0,2},{1,31},{2,4},{3,1},{4,6},{5,3},{6,8},{7,5},{8,10},{9,7},{10,... | collective-permute-start | bytes 1425416 | tf_op jit(solution)/shard_map/ppermute | solution.py:39
  31.5 10.8 %collective-permute-start.7 = (bf16[64,3712]{1,0:T(8,128)(2,1)S(1)}, bf16[64,3712]{1,0:T(8,128)(2,1)S(1)}, u32[]{:S(2)}, u32[]{:S(2)}) collective-permute-start(bf16[64,3712]{1,0:T(8,128)(2,1)S(1)} %collective-permute-done.6.refs_1_), channel_id=1, source_target_pairs={{0,2},{1,31},{2,4},{3,1},{4,6},{5,3},{6,8},{7,5},{8,10},{9,7},{10,... | collective-permute-start | bytes 1425416 | tf_op jit(solution)/shard_map/ppermute | solution.py:39
  42.3 11.2 %collective-permute-start.8 = (bf16[64,3712]{1,0:T(8,128)(2,1)S(1)}, bf16[64,3712]{1,0:T(8,128)(2,1)S(1)}, u32[]{:S(2)}, u32[]{:S(2)}) collective-permute-start(bf16[64,3712]{1,0:T(8,128)(2,1)S(1)} %collective-permute-done.7.refs_3_), channel_id=1, source_target_pairs={{0,2},{1,31},{2,4},{3,1},{4,6},{5,3},{6,8},{7,5},{8,10},{9,7},{10,... | collective-permute-start | bytes 1425416 | tf_op jit(solution)/shard_map/ppermute | solution.py:39
  48.7 11.1 %collective-permute-start.4 = (bf16[64,3712]{1,0:T(8,128)(2,1)S(1)}, bf16[64,3712]{1,0:T(8,128)(2,1)S(1)}, u32[]{:S(2)}, u32[]{:S(2)}) collective-permute-start(bf16[64,3712]{1,0:T(8,128)(2,1)S(1)} %collective-permute-done.3.refs_0_), channel_id=1, source_target_pairs={{0,2},{1,31},{2,4},{3,1},{4,6},{5,3},{6,8},{7,5},{8,10},{9,7},{10,... | collective-permute-start | bytes 1425416 | tf_op jit(solution)/shard_map/ppermute | solution.py:39
  59.8 15.6 %collective-permute-start.5 = (bf16[48,3712]{1,0:T(8,128)(2,1)S(1)}, bf16[48,3712]{1,0:T(8,128)(2,1)S(1)}, u32[]{:S(2)}, u32[]{:S(2)}) collective-permute-start(bf16[48,3712]{1,0:T(8,128)(2,1)S(1)} %slice.113), channel_id=1, source_target_pairs={{0,2},{1,31},{2,4},{3,1},{4,6},{5,3},{6,8},{7,5},{8,10},{9,7},{10,... | collective-permute-start | bytes 1069064 | tf_op jit(solution)/shard_map/ppermute | solution.py:39
  63.7 13.6 %collective-permute-start.10 = (bf16[48,3712]{1,0:T(8,128)(2,1)S(1)}, bf16[48,3712]{1,0:T(8,128)(2,1)S(1)}, u32[]{:S(2)}, u32[]{:S(2)}) collective-permute-start(bf16[48,3712]{1,0:T(8,128)(2,1)S(1)} %slice.115), channel_id=1, source_target_pairs={{0,2},{1,31},{2,4},{3,1},{4,6},{5,3},{6,8},{7,5},{8,10},{9,7},{10,... | collective-permute-start | bytes 1069064 | tf_op jit(solution)/shard_map/ppermute | solution.py:39
  77.4 15.1 %collective-permute-start.15 = (bf16[48,3712]{1,0:T(8,128)(2,1)S(1)}, bf16[48,3712]{1,0:T(8,128)(2,1)S(1)}, u32[]{:S(2)}, u32[]{:S(2)}) collective-permute-start(bf16[48,3712]{1,0:T(8,128)(2,1)S(1)} %collective-permute-done.10.refs_3_), channel_id=1, source_target_pairs={{0,2},{1,31},{2,4},{3,1},{4,6},{5,3},{6,8},{7,5},{8,10},{9,7},{10,... | collective-permute-start | bytes 1069064 | tf_op jit(solution)/shard_map/ppermute | solution.py:39
  84.0 17.7 %collective-permute-start.16 = (bf16[24,3712]{1,0:T(8,128)(2,1)S(1)}, bf16[24,3712]{1,0:T(8,128)(2,1)S(1)}, u32[]{:S(2)}, u32[]{:S(2)}) collective-permute-start(bf16[24,3712]{1,0:T(8,128)(2,1)S(1)} %slice.94), channel_id=1, source_target_pairs={{0,2},{1,31},{2,4},{3,1},{4,6},{5,3},{6,8},{7,5},{8,10},{9,7},{10,... | collective-permute-start | bytes 534536 | tf_op jit(solution)/shard_map/ppermute | solution.py:39
  87.7 13.9 %collective-permute-start.18 = (bf16[24,3712]{1,0:T(8,128)(2,1)S(1)}, bf16[24,3712]{1,0:T(8,128)(2,1)S(1)}, u32[]{:S(2)}, u32[]{:S(2)}) collective-permute-start(bf16[24,3712]{1,0:T(8,128)(2,1)S(1)} %slice.94), channel_id=1, source_target_pairs={{1,29},{2,6},{5,1},{6,10},{9,5},{10,14},{13,9},{14,18},{17,13},{18... | collective-permute-start | bytes 534536 | tf_op jit(solution)/shard_map/ppermute | solution.py:39
  139.7 10.7 %collective-permute-start.24 = (bf16[64,3584]{1,0:T(8,128)(2,1)S(1)}, bf16[64,3584]{1,0:T(8,128)(2,1)S(1)}, u32[]{:S(2)}, u32[]{:S(2)}) collective-permute-start(bf16[64,3584]{1,0:T(8,128)(2,1)S(1)} %add_convert_fusion.17), channel_id=1, source_target_pairs={{2,0},{31,1},{4,2},{1,3},{6,4},{3,5},{8,6},{5,7},{10,8},{7,9},{12,... | collective-permute-start | bytes 1376264 | tf_op jit(solution)/shard_map/ppermute | solution.py:39
  182.8 14.3 %collective-permute-start.36 = (bf16[2,32,3584]{2,1,0:T(8,128)(2,1)S(1)}, bf16[2,32,3584]{2,1,0:T(8,128)(2,1)}, u32[]{:S(2)}, u32[]{:S(2)}) collective-permute-start(bf16[2,32,3584]{2,1,0:T(8,128)(2,1)S(1)} %slice.117), channel_id=1, source_target_pairs={{0,1},{1,0},{2,3},{3,2},{4,5},{5,4},{6,7},{7,6},{8,9},{9,8},{10,11... | collective-permute-start | bytes 1376264 | tf_op jit(solution)/shard_map/ppermute | solution.py:24
  219.7 11.0 %collective-permute-start.40 = (bf16[64,3712]{1,0:T(8,128)(2,1)S(1)}, bf16[64,3712]{1,0:T(8,128)(2,1)S(1)}, u32[]{:S(2)}, u32[]{:S(2)}) collective-permute-start(bf16[64,3712]{1,0:T(8,128)(2,1)S(1)} %get-tuple-element.102), channel_id=1, source_target_pairs={{0,2},{1,31},{2,4},{3,1},{4,6},{5,3},{6,8},{7,5},{8,10},{9,7},{10,... | collective-permute-start | bytes 1425416 | tf_op jit(solution)/shard_map/ppermute | solution.py:39
  241.4 16.6 %collective-permute-start.42 = (bf16[64,3712]{1,0:T(8,128)(2,1)S(1)}, bf16[64,3712]{1,0:T(8,128)(2,1)S(1)}, u32[]{:S(2)}, u32[]{:S(2)}) collective-permute-start(bf16[64,3712]{1,0:T(8,128)(2,1)S(1)} %collective-permute-done.41.refs_2_), channel_id=1, source_target_pairs={{0,2},{1,31},{2,4},{3,1},{4,6},{5,3},{6,8},{7,5},{8,10},{9,7},{10,... | collective-permute-start | bytes 1425416 | tf_op jit(solution)/shard_map/ppermute | solution.py:39
  246.5 13.4 %collective-permute-start.47 = (bf16[64,3712]{1,0:T(8,128)(2,1)S(1)}, bf16[64,3712]{1,0:T(8,128)(2,1)S(1)}, u32[]{:S(2)}, u32[]{:S(2)}) collective-permute-start(bf16[64,3712]{1,0:T(8,128)(2,1)S(1)} %collective-permute-done.44.refs_3_), channel_id=1, source_target_pairs={{0,2},{1,31},{2,4},{3,1},{4,6},{5,3},{6,8},{7,5},{8,10},{9,7},{10,... | collective-permute-start | bytes 1425416 | tf_op jit(solution)/shard_map/ppermute | solution.py:39
  259.9 12.8 %collective-permute-start.48 = (bf16[64,3712]{1,0:T(8,128)(2,1)S(1)}, bf16[64,3712]{1,0:T(8,128)(2,1)S(1)}, u32[]{:S(2)}, u32[]{:S(2)}) collective-permute-start(bf16[64,3712]{1,0:T(8,128)(2,1)S(1)} %collective-permute-done.47.refs_1_), channel_id=1, source_target_pairs={{0,2},{1,31},{2,4},{3,1},{4,6},{5,3},{6,8},{7,5},{8,10},{9,7},{10,... | collective-permute-start | bytes 1425416 | tf_op jit(solution)/shard_map/ppermute | solution.py:39
  267.7 12.3 %collective-permute-start.46 = (bf16[48,3712]{1,0:T(8,128)(2,1)S(1)}, bf16[48,3712]{1,0:T(8,128)(2,1)S(1)}, u32[]{:S(2)}, u32[]{:S(2)}) collective-permute-start(bf16[48,3712]{1,0:T(8,128)(2,1)S(1)} %slice.122), channel_id=1, source_target_pairs={{0,2},{1,31},{2,4},{3,1},{4,6},{5,3},{6,8},{7,5},{8,10},{9,7},{10,... | collective-permute-start | bytes 1069064 | tf_op jit(solution)/shard_map/ppermute | solution.py:39
  281.9 14.1 %collective-permute-start.51 = (bf16[48,3712]{1,0:T(8,128)(2,1)S(1)}, bf16[48,3712]{1,0:T(8,128)(2,1)S(1)}, u32[]{:S(2)}, u32[]{:S(2)}) collective-permute-start(bf16[48,3712]{1,0:T(8,128)(2,1)S(1)} %collective-permute-done.49.refs_3_), channel_id=1, source_target_pairs={{0,2},{1,31},{2,4},{3,1},{4,6},{5,3},{6,8},{7,5},{8,10},{9,7},{10,... | collective-permute-start | bytes 1069064 | tf_op jit(solution)/shard_map/ppermute | solution.py:39
  288.4 17.7 %collective-permute-start.52 = (bf16[24,3712]{1,0:T(8,128)(2,1)S(1)}, bf16[24,3712]{1,0:T(8,128)(2,1)S(1)}, u32[]{:S(2)}, u32[]{:S(2)}) collective-permute-start(bf16[24,3712]{1,0:T(8,128)(2,1)S(1)} %slice.124), channel_id=1, source_target_pairs={{0,2},{1,31},{2,4},{3,1},{4,6},{5,3},{6,8},{7,5},{8,10},{9,7},{10,... | collective-permute-start | bytes 534536 | tf_op jit(solution)/shard_map/ppermute | solution.py:39
  291.3 14.9 %collective-permute-start.54 = (bf16[24,3712]{1,0:T(8,128)(2,1)S(1)}, bf16[24,3712]{1,0:T(8,128)(2,1)S(1)}, u32[]{:S(2)}, u32[]{:S(2)}) collective-permute-start(bf16[24,3712]{1,0:T(8,128)(2,1)S(1)} %slice.124), channel_id=1, source_target_pairs={{1,29},{2,6},{5,1},{6,10},{9,5},{10,14},{13,9},{14,18},{17,13},{18... | collective-permute-start | bytes 534536 | tf_op jit(solution)/shard_map/ppermute | solution.py:39
  343.4 10.7 %collective-permute-start.60 = (bf16[64,3584]{1,0:T(8,128)(2,1)S(1)}, bf16[64,3584]{1,0:T(8,128)(2,1)S(1)}, u32[]{:S(2)}, u32[]{:S(2)}) collective-permute-start(bf16[64,3584]{1,0:T(8,128)(2,1)S(1)} %add_convert_fusion.8), channel_id=1, source_target_pairs={{2,0},{31,1},{4,2},{1,3},{6,4},{3,5},{8,6},{5,7},{10,8},{7,9},{12,... | collective-permute-start | bytes 1376264 | tf_op jit(solution)/shard_map/ppermute | solution.py:39
  386.5 13.8 %collective-permute-start.72 = (bf16[2,32,3584]{2,1,0:T(8,128)(2,1)S(1)}, bf16[2,32,3584]{2,1,0:T(8,128)(2,1)S(1)}, u32[]{:S(2)}, u32[]{:S(2)}) collective-permute-start(bf16[2,32,3584]{2,1,0:T(8,128)(2,1)S(1)} %slice.127), channel_id=1, source_target_pairs={{0,1},{1,0},{2,3},{3,2},{4,5},{5,4},{6,7},{7,6},{8,9},{9,8},{10,11... | collective-permute-start | bytes 1376264 | tf_op jit(solution)/shard_map/ppermute | solution.py:24
  (85 other events, 1189.1 us)

commit v3 on v0

--- a/solution.py
+++ b/solution.py
@@ -151,7 +151,8 @@
     def whole(shape):
         return pl.BlockSpec(shape, lambda g, s: (0,) * len(shape), pipeline_mode=once)
 
-    outs = [jax.ShapeDtypeStruct((x.shape[0], width), jnp.bfloat16) for x in xs]
+    kind = pltpu.HBM if step_now else jax.ShapeDtypeStruct
+    outs = [kind((x.shape[0], width), jnp.bfloat16) for x in xs]
     sums = pl.pallas_call(
         functools.partial(expert_kernel, len(blocks)),
         out_shape=outs,
@@ -176,6 +177,10 @@
     return [sums[2 * i : 2 * i + 2] for i in range(len(blocks))]
 
 
+def after(blocks, sums):
+    return [lax.optimization_barrier((block, sums))[0] for block in blocks]
+
+
 def add_rows(own, arrived):
     short = own.shape[0] - arrived.shape[0]
     arrived = jnp.pad(arrived.astype(jnp.float32), ((0, short), (0, 0)))
@@ -215,28 +220,33 @@
         def compute(blocks, wait_for=None):
             return expert_rows(step_now, expert, blocks, pre, down, up, wait_for)
 
+        ends = () if step_now == 0 else (half - 5, half - 3)
         streams = [payload[lane] for lane in range(lanes)]
-        blocks = [(chip, mine)]
+        blocks, partials = [(chip, mine)], []
         for distance, size in enumerate(sizes, 1):
             far = distance == half
             arrived = [hop(s[:size], True, 2 if far else 1) for s in streams]
             blocks.append((lax.rem(chips + chip - way * distance, chips), arrived))
+            if distance in ends:
+                done = len(partials)
+                partials += compute(blocks[done : done + (2 if done else 3)])
+                arrived = after(arrived, partials[-1][1])
             if distance < half - 1:
                 streams = arrived
-        last = compute(blocks[half - 1 :])
-        own, *late = compute([blocks[0], *blocks[half - 3 : half - 1]])
+        partials = partials or [None] * (half - 3)
+        partials += compute(blocks[half - 3 :])
         sums = [
-            add_rows(add_rows(o, hop(t, False)), hop(u, False, 2)) for o, t, u in zip(late[1], *last)
+            add_rows(add_rows(o, hop(t, False)), hop(u, False, 2))
+            for o, t, u in zip(*partials[half - 2 :])
         ]
-        partials = {half - 3: late[0]}
         for distance in range(half - 2, 0, -1):
-            if distance - 1 not in partials and distance > 1:
-                partials[distance - 2], partials[distance - 1] = compute(
-                    blocks[distance - 2 : distance], sums[0]
-                )
+            if distance > 1 and partials[distance - 1] is None:
+                done = 3 * (distance // 4)
+                partials[done:distance] = compute(blocks[done:distance], sums[0])
             sums = [hop(s, False) for s in sums]
             if distance > 1:
                 sums = [add_rows(o, s) for o, s in zip(partials[distance - 1], sums)]
+        own = partials[0]
         arrived = jnp.einsum(
             "kpr,kpd->krd", sorting, jnp.stack(sums), preferred_element_type=jnp.float32
         ).astype(jnp.bfloat16)

time: 404 us -> 405 us (level)
  starting transfers between devices: 268 us -> 232 us
  waiting for transfers between devices: 84.4 us -> 114 us
  local copies, waits for them, and re-layouts: 4.49 us -> 10 us
    ppermute x64, starting transfers between devices: 222 us -> 190 us  [hop(): return lax.ppermute(block, 'expert', route)]
    ppermute x64, waiting for transfers between devices: 70.8 us -> 100 us  [hop(): return lax.ppermute(block, 'expert', route)]
    pallas_call x8 -> x6, Pallas kernels: 25.7 us -> 25.7 us  [expert_rows(): pl.pallas_call(functools.partial(expert_kernel, len(blocks)), out_shape=o...]
  transfers between devices with their start and end apart: 73 -> 73, of which waited for: 44 -> 45; matrix products, arithmetic and copies ran while one was open for 3% -> 3% of each run, Pallas kernels for 5% -> 4%
where the time goes in v3:
time: 405 us; the launch traced here: 402 us
  starting transfers between devices  232 us (57%)
  waiting for transfers between devices  114 us (28%)
  Pallas kernels  25.7 us (6%)
  other arithmetic  15.8 us (4%)
  local copies, waits for them, and re-layouts  10 us (2%)
    ppermute x64, starting transfers between devices, hop(): return lax.ppermute(block, 'expert', route)  190 us
    ppermute x64, waiting for transfers between devices, hop(): return lax.ppermute(block, 'expert', route)  100 us
    ppermute x7, starting transfers between devices, swap_cores(): return lax.ppermute(block, 'expert', [(i, i ^ 1) for i in devices])  36.3 us
    pallas_call x6, Pallas kernels, expert_rows(): pl.pallas_call(functools.partial(expert_kernel, len(blocks)), out_shape=o...  25.7 us
    ppermute x2, waiting for transfers between devices, from_behind(): return lax.ppermute(block, axis, route)  8.45 us
  transfers between devices with their start and end apart: 73, of which 45 were waited for; matrix products, arithmetic and copies ran while one was open for 3% of the time, Pallas kernels for 4%

profile of v3, /device:TPU:25, one launch (start us, length us, event | category | flops | bytes accessed | tf_op | source)
XLA Modules:
  0.0 402.2 jit_solution(18382441369113782661)
XLA Ops:
  8.7 11.1 %collective-permute-start.6 = (bf16[64,3712]{1,0:T(8,128)(2,1)S(1)}, bf16[64,3712]{1,0:T(8,128)(2,1)S(1)}, u32[]{:S(2)}, u32[]{:S(2)}) collective-permute-start(bf16[64,3712]{1,0:T(8,128)(2,1)S(1)} %get-tuple-element.95), channel_id=1, source_target_pairs={{0,2},{1,31},{2,4},{3,1},{4,6},{5,3},{6,8},{7,5},{8,10},{9,7},{10,... | collective-permute-start | bytes 1425416 | tf_op jit(solution)/shard_map/ppermute | solution.py:39
  25.4 5.0 %collective-permute-start.7 = (bf16[64,3712]{1,0:T(8,128)(2,1)S(1)}, bf16[64,3712]{1,0:T(8,128)(2,1)S(1)}, u32[]{:S(2)}, u32[]{:S(2)}) collective-permute-start(bf16[64,3712]{1,0:T(8,128)(2,1)S(1)} %collective-permute-done.6.refs_3_), channel_id=1, source_target_pairs={{0,2},{1,31},{2,4},{3,1},{4,6},{5,3},{6,8},{7,5},{8,10},{9,7},{10,... | collective-permute-start | bytes 1425416 | tf_op jit(solution)/shard_map/ppermute | solution.py:39
  30.5 5.0 %collective-permute-start.2 = (bf16[64,3712]{1,0:T(8,128)(2,1)S(1)}, bf16[64,3712]{1,0:T(8,128)(2,1)S(1)}, u32[]{:S(2)}, u32[]{:S(2)}) collective-permute-start(bf16[64,3712]{1,0:T(8,128)(2,1)S(1)} %collective-permute-done.1.refs_2_), channel_id=1, source_target_pairs={{0,2},{1,31},{2,4},{3,1},{4,6},{5,3},{6,8},{7,5},{8,10},{9,7},{10,... | collective-permute-start | bytes 1425416 | tf_op jit(solution)/shard_map/ppermute | solution.py:39
  48.8 4.6 %collective-permute-start.9 = (bf16[64,3712]{1,0:T(8,128)(2,1)S(1)}, bf16[64,3712]{1,0:T(8,128)(2,1)S(1)}, u32[]{:S(2)}, u32[]{:S(2)}) collective-permute-start(bf16[64,3712]{1,0:T(8,128)(2,1)S(1)} %collective-permute-done.8.refs_1_), channel_id=1, source_target_pairs={{0,2},{1,31},{2,4},{3,1},{4,6},{5,3},{6,8},{7,5},{8,10},{9,7},{10,... | collective-permute-start | bytes 1425416 | tf_op jit(solution)/shard_map/ppermute | solution.py:39
  60.3 4.8 %collective-permute-start.10 = (bf16[48,3712]{1,0:T(8,128)(2,1)}, bf16[48,3712]{1,0:T(8,128)(2,1)}, u32[]{:S(2)}, u32[]{:S(2)}) collective-permute-start(bf16[48,3712]{1,0:T(8,128)(2,1)} %slice.115), channel_id=1, source_target_pairs={{0,2},{1,31},{2,4},{3,1},{4,6},{5,3},{6,8},{7,5},{8,10},{9,7},{10,... | collective-permute-start | bytes 1069064 | tf_op jit(solution)/shard_map/ppermute | solution.py:39
  74.8 4.7 %collective-permute-start.11 = (bf16[48,3712]{1,0:T(8,128)(2,1)}, bf16[48,3712]{1,0:T(8,128)(2,1)S(1)}, u32[]{:S(2)}, u32[]{:S(2)}) collective-permute-start(bf16[48,3712]{1,0:T(8,128)(2,1)} %collective-permute-done.5.refs_0_), channel_id=1, source_target_pairs={{0,2},{1,31},{2,4},{3,1},{4,6},{5,3},{6,8},{7,5},{8,10},{9,7},{10,... | collective-permute-start | bytes 1069064 | tf_op jit(solution)/shard_map/ppermute | solution.py:39
  86.5 5.7 %collective-permute-start.15 = (bf16[24,3712]{1,0:T(8,128)(2,1)S(1)}, bf16[24,3712]{1,0:T(8,128)(2,1)S(1)}, u32[]{:S(2)}, u32[]{:S(2)}) collective-permute-start(bf16[24,3712]{1,0:T(8,128)(2,1)S(1)} %slice.116), channel_id=1, source_target_pairs={{1,29},{2,6},{5,1},{6,10},{9,5},{10,14},{13,9},{14,18},{17,13},{18... | collective-permute-start | bytes 534536 | tf_op jit(solution)/shard_map/ppermute | solution.py:39
  98.7 4.6 %shard_map.73 = (bf16[48,3584]{1,0:T(8,128)(2,1)S(1)}, bf16[48,3584]{1,0:T(8,128)(2,1)S(1)}, bf16[48,3584]{1,0:T(8,128)(2,1)S(1)}, bf16[48,3584]{1,0:T(8,128)(2,...) custom-call(s32[5]{0:T(128)S(1)} %stack.113.where_ref, ...), custom_call_target="tpu_custom_call" | custom-call | flops 2113929216 | bytes 11468800 | tf_op jit(solution)/shard_map/pallas_call | solution.py:156
  174.9 5.0 %collective-permute-done.35 = bf16[64,3584]{1,0:T(8,128)(2,1)S(1)} collective-permute-done((bf16[64,3584]{1,0:T(8,128)(2,1)S(1)}, bf16[64,3584]{1,0:T(8,128)(2,1)S(1)}, u32[]{:S(2)}, u32[]{:S(2)}) %collective-permute-start.35) | collective-permute-done | bytes 458784 | tf_op jit(solution)/shard_map/ppermute | solution.py:39
  181.1 11.9 %collective-permute-start.36 = (bf16[2,32,3584]{2,1,0:T(8,128)(2,1)}, bf16[2,32,3584]{2,1,0:T(8,128)(2,1)}, u32[]{:S(2)}, u32[]{:S(2)}) collective-permute-start(bf16[2,32,3584]{2,1,0:T(8,128)(2,1)} %slice.119), channel_id=1, source_target_pairs={{0,1},{1,0},{2,3},{3,2},{4,5},{5,4},{6,7},{7,6},{8,9},{9,8},{10,11... | collective-permute-start | bytes 1376264 | tf_op jit(solution)/shard_map/ppermute | solution.py:24
  196.1 4.6 %collective-permute-start.37 = (bf16[32,3584]{1,0:T(8,128)(2,1)S(1)}, bf16[32,3584]{1,0:T(8,128)(2,1)S(1)}, u32[]{:S(2)}, u32[]{:S(2)}) collective-permute-start(bf16[32,3584]{1,0:T(8,128)(2,1)S(1)} %get-tuple-element.103), channel_id=1, source_target_pairs={{32,0},{64,32},{96,64},{128,96},{160,128},{192,160},{224,192},{256... | collective-permute-start | bytes 688136 | tf_op jit(solution)/shard_map/ppermute | solution.py:19
  205.2 5.9 %collective-permute-done.38 = bf16[32,3584]{1,0:T(8,128)(2,1)S(1)} collective-permute-done((bf16[32,3584]{1,0:T(8,128)(2,1)S(1)}, bf16[32,3584]{1,0:T(8,128)(2,1)S(1)}, u32[]{:S(2)}, u32[]{:S(2)}) %collective-permute-start.38) | collective-permute-done | bytes 229408 | tf_op jit(solution)/shard_map/ppermute | solution.py:19
  218.8 4.8 %collective-permute-start.41 = (bf16[64,3712]{1,0:T(8,128)(2,1)S(1)}, bf16[64,3712]{1,0:T(8,128)(2,1)S(1)}, u32[]{:S(2)}, u32[]{:S(2)}) collective-permute-start(bf16[64,3712]{1,0:T(8,128)(2,1)S(1)} %get-tuple-element.93), channel_id=1, source_target_pairs={{0,2},{1,31},{2,4},{3,1},{4,6},{5,3},{6,8},{7,5},{8,10},{9,7},{10,... | collective-permute-start | bytes 1425416 | tf_op jit(solution)/shard_map/ppermute | solution.py:39
  229.2 5.0 %collective-permute-start.43 = (bf16[64,3712]{1,0:T(8,128)(2,1)S(1)}, bf16[64,3712]{1,0:T(8,128)(2,1)S(1)}, u32[]{:S(2)}, u32[]{:S(2)}) collective-permute-start(bf16[64,3712]{1,0:T(8,128)(2,1)S(1)} %collective-permute-done.41.refs_3_), channel_id=1, source_target_pairs={{0,2},{1,31},{2,4},{3,1},{4,6},{5,3},{6,8},{7,5},{8,10},{9,7},{10,... | collective-permute-start | bytes 1425416 | tf_op jit(solution)/shard_map/ppermute | solution.py:39
  234.3 5.0 %collective-permute-start.42 = (bf16[64,3712]{1,0:T(8,128)(2,1)S(1)}, bf16[64,3712]{1,0:T(8,128)(2,1)S(1)}, u32[]{:S(2)}, u32[]{:S(2)}) collective-permute-start(bf16[64,3712]{1,0:T(8,128)(2,1)S(1)} %collective-permute-done.40.refs_2_), channel_id=1, source_target_pairs={{0,2},{1,31},{2,4},{3,1},{4,6},{5,3},{6,8},{7,5},{8,10},{9,7},{10,... | collective-permute-start | bytes 1425416 | tf_op jit(solution)/shard_map/ppermute | solution.py:39
  239.8 5.0 %collective-permute-start.45 = (bf16[64,3712]{1,0:T(8,128)(2,1)S(1)}, bf16[64,3712]{1,0:T(8,128)(2,1)S(1)}, u32[]{:S(2)}, u32[]{:S(2)}) collective-permute-start(bf16[64,3712]{1,0:T(8,128)(2,1)S(1)} %collective-permute-done.43.refs_5_), channel_id=1, source_target_pairs={{0,2},{1,31},{2,4},{3,1},{4,6},{5,3},{6,8},{7,5},{8,10},{9,7},{10,... | collective-permute-start | bytes 1425416 | tf_op jit(solution)/shard_map/ppermute | solution.py:39
  244.9 5.0 %collective-permute-start.44 = (bf16[64,3712]{1,0:T(8,128)(2,1)S(1)}, bf16[64,3712]{1,0:T(8,128)(2,1)S(1)}, u32[]{:S(2)}, u32[]{:S(2)}) collective-permute-start(bf16[64,3712]{1,0:T(8,128)(2,1)S(1)} %collective-permute-done.42.refs_4_), channel_id=1, source_target_pairs={{0,2},{1,31},{2,4},{3,1},{4,6},{5,3},{6,8},{7,5},{8,10},{9,7},{10,... | collective-permute-start | bytes 1425416 | tf_op jit(solution)/shard_map/ppermute | solution.py:39
  252.0 5.1 %shard_map.76 = (bf16[32,3584]{1,0:T(8,128)(2,1)}, bf16[32,3584]{1,0:T(8,128)(2,1)}, bf16[64,3584]{1,0:T(8,128)(2,1)}, bf16[64,3584]{1,0:T(8,128)(2,1)}, bf16[64...) custom-call(s32[4]{0:T(128)S(1)} %pad_add_fusion.where_ref, bf16[32,3712]{1,0:T(8,128)(2,1)S(1)} %get-tuple-element.98.refs_0_, ...), custom_call_target="tpu_custom_call" | custom-call | flops 2348810240 | bytes 11927552 | tf_op jit(solution)/shard_map/pallas_call | solution.py:156
  260.9 5.8 %collective-permute-done.47.refs_3_ = bf16[64,3712]{1,0:T(8,128)(2,1)S(1)} collective-permute-done((bf16[64,3712]{1,0:T(8,128)(2,1)S(1)}, bf16[64,3712]{1,0:T(8,128)(2,1)S(1)}, u32[]{:S(2)}, u32[]{:S(2)}) %collective-permute-start.47) | collective-permute-done | bytes 475168 | tf_op jit(solution)/shard_map/ppermute | solution.py:39
  293.1 4.8 %collective-permute-start.54 = (bf16[24,3712]{1,0:T(8,128)(2,1)S(1)}, bf16[24,3712]{1,0:T(8,128)(2,1)S(1)}, u32[]{:S(2)}, u32[]{:S(2)}) collective-permute-start(bf16[24,3712]{1,0:T(8,128)(2,1)S(1)} %slice.126), channel_id=1, source_target_pairs={{1,29},{2,6},{5,1},{6,10},{9,5},{10,14},{13,9},{14,18},{17,13},{18... | collective-permute-start | bytes 534536 | tf_op jit(solution)/shard_map/ppermute | solution.py:39
  304.1 4.8 %shard_map.78 = (bf16[48,3584]{1,0:T(8,128)(2,1)}, bf16[48,3584]{1,0:T(8,128)(2,1)}, bf16[48,3584]{1,0:T(8,128)(2,1)}, bf16[48,3584]{1,0:T(8,128)(2,1)}, bf16[24...) custom-call(s32[5]{0:T(128)S(1)} %stack.113.where_ref, ...), custom_call_target="tpu_custom_call" | custom-call | flops 2113929216 | bytes 11468800 | tf_op jit(solution)/shard_map/pallas_call | solution.py:156
  345.1 4.7 %collective-permute-done.60 = bf16[64,3584]{1,0:T(8,128)(2,1)S(1)} collective-permute-done((bf16[64,3584]{1,0:T(8,128)(2,1)S(1)}, bf16[64,3584]{1,0:T(8,128)(2,1)S(1)}, u32[]{:S(2)}, u32[]{:S(2)}) %collective-permute-start.60) | collective-permute-done | bytes 458784 | tf_op jit(solution)/shard_map/ppermute | solution.py:39
  381.7 5.1 %collective-permute-done.71 = bf16[64,3584]{1,0:T(8,128)(2,1)S(1)} collective-permute-done((bf16[64,3584]{1,0:T(8,128)(2,1)S(1)}, bf16[64,3584]{1,0:T(8,128)(2,1)S(1)}, u32[]{:S(2)}, u32[]{:S(2)}) %collective-permute-start.71) | collective-permute-done | bytes 458784 | tf_op jit(solution)/shard_map/ppermute | solution.py:39
  387.3 12.4 %collective-permute-start.72 = (bf16[2,32,3584]{2,1,0:T(8,128)(2,1)S(1)}, bf16[2,32,3584]{2,1,0:T(8,128)(2,1)S(1)}, u32[]{:S(2)}, u32[]{:S(2)}) collective-permute-start(bf16[2,32,3584]{2,1,0:T(8,128)(2,1)S(1)} %slice.129), channel_id=1, source_target_pairs={{0,1},{1,0},{2,3},{3,2},{4,5},{5,4},{6,7},{7,6},{8,9},{9,8},{10,11... | collective-permute-start | bytes 1376264 | tf_op jit(solution)/shard_map/ppermute | solution.py:24
  (298 shorter events, 260.2 us)
Async XLA Ops:
  8.7 16.7 %collective-permute-start.6 = (bf16[64,3712]{1,0:T(8,128)(2,1)S(1)}, bf16[64,3712]{1,0:T(8,128)(2,1)S(1)}, u32[]{:S(2)}, u32[]{:S(2)}) collective-permute-start(bf16[64,3712]{1,0:T(8,128)(2,1)S(1)} %get-tuple-element.95), channel_id=1, source_target_pairs={{0,2},{1,31},{2,4},{3,1},{4,6},{5,3},{6,8},{7,5},{8,10},{9,7},{10,... | collective-permute-start | bytes 1425416 | tf_op jit(solution)/shard_map/ppermute | solution.py:39
  25.4 12.9 %collective-permute-start.7 = (bf16[64,3712]{1,0:T(8,128)(2,1)S(1)}, bf16[64,3712]{1,0:T(8,128)(2,1)S(1)}, u32[]{:S(2)}, u32[]{:S(2)}) collective-permute-start(bf16[64,3712]{1,0:T(8,128)(2,1)S(1)} %collective-permute-done.6.refs_3_), channel_id=1, source_target_pairs={{0,2},{1,31},{2,4},{3,1},{4,6},{5,3},{6,8},{7,5},{8,10},{9,7},{10,... | collective-permute-start | bytes 1425416 | tf_op jit(solution)/shard_map/ppermute | solution.py:39
  30.5 12.0 %collective-permute-start.2 = (bf16[64,3712]{1,0:T(8,128)(2,1)S(1)}, bf16[64,3712]{1,0:T(8,128)(2,1)S(1)}, u32[]{:S(2)}, u32[]{:S(2)}) collective-permute-start(bf16[64,3712]{1,0:T(8,128)(2,1)S(1)} %collective-permute-done.1.refs_2_), channel_id=1, source_target_pairs={{0,2},{1,31},{2,4},{3,1},{4,6},{5,3},{6,8},{7,5},{8,10},{9,7},{10,... | collective-permute-start | bytes 1425416 | tf_op jit(solution)/shard_map/ppermute | solution.py:39
  36.3 43.2 %collective-permute-start.19 = (bf16[3584,256]{1,0:T(8,128)(2,1)}, bf16[3584,256]{1,0:T(8,128)(2,1)}, u32[]{:S(2)}, u32[]{:S(2)}) collective-permute-start(bf16[3584,256]{1,0:T(8,128)(2,1)} %bitcast.20), channel_id=1, source_target_pairs={{0,1},{1,0},{2,3},{3,2},{4,5},{5,4},{6,7},{7,6},{8,9},{9,8},{10,11... | collective-permute-start | bytes 5505032 | tf_op jit(solution)/shard_map/ppermute | solution.py:24
  42.5 10.9 %collective-permute-start.3 = (bf16[64,3712]{1,0:T(8,128)(2,1)S(1)}, bf16[64,3712]{1,0:T(8,128)(2,1)S(1)}, u32[]{:S(2)}, u32[]{:S(2)}) collective-permute-start(bf16[64,3712]{1,0:T(8,128)(2,1)S(1)} %collective-permute-done.2.refs_4_), channel_id=1, source_target_pairs={{0,2},{1,31},{2,4},{3,1},{4,6},{5,3},{6,8},{7,5},{8,10},{9,7},{10,... | collective-permute-start | bytes 1425416 | tf_op jit(solution)/shard_map/ppermute | solution.py:39
  46.9 47.3 %collective-permute-start.18 = (bf16[256,3584]{1,0:T(8,128)(2,1)}, bf16[256,3584]{1,0:T(8,128)(2,1)}, u32[]{:S(2)}, u32[]{:S(2)}) collective-permute-start(bf16[256,3584]{1,0:T(8,128)(2,1)} %bitcast.19), channel_id=1, source_target_pairs={{0,1},{1,0},{2,3},{3,2},{4,5},{5,4},{6,7},{7,6},{8,9},{9,8},{10,11... | collective-permute-start | bytes 5505032 | tf_op jit(solution)/shard_map/ppermute | solution.py:24
  53.4 11.7 %collective-permute-start.4 = (bf16[64,3712]{1,0:T(8,128)(2,1)S(1)}, bf16[64,3712]{1,0:T(8,128)(2,1)S(1)}, u32[]{:S(2)}, u32[]{:S(2)}) collective-permute-start(bf16[64,3712]{1,0:T(8,128)(2,1)S(1)} %collective-permute-done.3.refs_0_), channel_id=1, source_target_pairs={{0,2},{1,31},{2,4},{3,1},{4,6},{5,3},{6,8},{7,5},{8,10},{9,7},{10,... | collective-permute-start | bytes 1425416 | tf_op jit(solution)/shard_map/ppermute | solution.py:39
  57.4 12.7 %collective-permute-start.17 = (bf16[2,2,384,256]{3,2,1,0:T(8,128)(2,1)}, bf16[2,2,384,256]{3,2,1,0:T(8,128)(2,1)}, u32[]{:S(2)}, u32[]{:S(2)}) collective-permute-start(bf16[2,2,384,256]{3,2,1,0:T(8,128)(2,1)} %bitcast.17), channel_id=1, source_target_pairs={{0,1},{1,0},{2,3},{3,2},{4,5},{5,4},{6,7},{7,6},{8,9},{9,8},{10,11... | collective-permute-start | bytes 2359304 | tf_op jit(solution)/shard_map/ppermute | solution.py:24
  60.3 11.3 %collective-permute-start.10 = (bf16[48,3712]{1,0:T(8,128)(2,1)}, bf16[48,3712]{1,0:T(8,128)(2,1)}, u32[]{:S(2)}, u32[]{:S(2)}) collective-permute-start(bf16[48,3712]{1,0:T(8,128)(2,1)} %slice.115), channel_id=1, source_target_pairs={{0,2},{1,31},{2,4},{3,1},{4,6},{5,3},{6,8},{7,5},{8,10},{9,7},{10,... | collective-permute-start | bytes 1069064 | tf_op jit(solution)/shard_map/ppermute | solution.py:39
  74.8 11.7 %collective-permute-start.11 = (bf16[48,3712]{1,0:T(8,128)(2,1)}, bf16[48,3712]{1,0:T(8,128)(2,1)S(1)}, u32[]{:S(2)}, u32[]{:S(2)}) collective-permute-start(bf16[48,3712]{1,0:T(8,128)(2,1)} %collective-permute-done.5.refs_0_), channel_id=1, source_target_pairs={{0,2},{1,31},{2,4},{3,1},{4,6},{5,3},{6,8},{7,5},{8,10},{9,7},{10,... | collective-permute-start | bytes 1069064 | tf_op jit(solution)/shard_map/ppermute | solution.py:39
  81.9 14.6 %collective-permute-start.16 = (bf16[24,3712]{1,0:T(8,128)(2,1)S(1)}, bf16[24,3712]{1,0:T(8,128)(2,1)S(1)}, u32[]{:S(2)}, u32[]{:S(2)}) collective-permute-start(bf16[24,3712]{1,0:T(8,128)(2,1)S(1)} %slice.117), channel_id=1, source_target_pairs={{1,29},{2,6},{5,1},{6,10},{9,5},{10,14},{13,9},{14,18},{17,13},{18... | collective-permute-start | bytes 534536 | tf_op jit(solution)/shard_map/ppermute | solution.py:39
  84.5 11.9 %collective-permute-start.14 = (bf16[24,3712]{1,0:T(8,128)(2,1)S(1)}, bf16[24,3712]{1,0:T(8,128)(2,1)S(1)}, u32[]{:S(2)}, u32[]{:S(2)}) collective-permute-start(bf16[24,3712]{1,0:T(8,128)(2,1)S(1)} %slice.117), channel_id=1, source_target_pairs={{0,2},{1,31},{2,4},{3,1},{4,6},{5,3},{6,8},{7,5},{8,10},{9,7},{10,... | collective-permute-start | bytes 534536 | tf_op jit(solution)/shard_map/ppermute | solution.py:39
  136.2 11.5 %collective-permute-start.32 = (bf16[64,3584]{1,0:T(8,128)(2,1)S(1)}, bf16[64,3584]{1,0:T(8,128)(2,1)S(1)}, u32[]{:S(2)}, u32[]{:S(2)}) collective-permute-start(bf16[64,3584]{1,0:T(8,128)(2,1)S(1)} %add_convert_fusion.13), channel_id=1, source_target_pairs={{2,0},{31,1},{4,2},{1,3},{6,4},{3,5},{8,6},{5,7},{10,8},{7,9},{12,... | collective-permute-start | bytes 1376264 | tf_op jit(solution)/shard_map/ppermute | solution.py:39
  142.9 10.8 %collective-permute-start.25 = (bf16[64,3584]{1,0:T(8,128)(2,1)S(1)}, bf16[64,3584]{1,0:T(8,128)(2,1)S(1)}, u32[]{:S(2)}, u32[]{:S(2)}) collective-permute-start(bf16[64,3584]{1,0:T(8,128)(2,1)S(1)} %add_convert_fusion.16), channel_id=1, source_target_pairs={{2,0},{31,1},{4,2},{1,3},{6,4},{3,5},{8,6},{5,7},{10,8},{7,9},{12,... | collective-permute-start | bytes 1376264 | tf_op jit(solution)/shard_map/ppermute | solution.py:39
  158.3 10.9 %collective-permute-start.34 = (bf16[64,3584]{1,0:T(8,128)(2,1)S(1)}, bf16[64,3584]{1,0:T(8,128)(2,1)S(1)}, u32[]{:S(2)}, u32[]{:S(2)}) collective-permute-start(bf16[64,3584]{1,0:T(8,128)(2,1)S(1)} %add_convert_fusion.11), channel_id=1, source_target_pairs={{2,0},{31,1},{4,2},{1,3},{6,4},{3,5},{8,6},{5,7},{10,8},{7,9},{12,... | collective-permute-start | bytes 1376264 | tf_op jit(solution)/shard_map/ppermute | solution.py:39
  181.1 13.7 %collective-permute-start.36 = (bf16[2,32,3584]{2,1,0:T(8,128)(2,1)}, bf16[2,32,3584]{2,1,0:T(8,128)(2,1)}, u32[]{:S(2)}, u32[]{:S(2)}) collective-permute-start(bf16[2,32,3584]{2,1,0:T(8,128)(2,1)} %slice.119), channel_id=1, source_target_pairs={{0,1},{1,0},{2,3},{3,2},{4,5},{5,4},{6,7},{7,6},{8,9},{9,8},{10,11... | collective-permute-start | bytes 1376264 | tf_op jit(solution)/shard_map/ppermute | solution.py:24
  239.8 17.3 %collective-permute-start.45 = (bf16[64,3712]{1,0:T(8,128)(2,1)S(1)}, bf16[64,3712]{1,0:T(8,128)(2,1)S(1)}, u32[]{:S(2)}, u32[]{:S(2)}) collective-permute-start(bf16[64,3712]{1,0:T(8,128)(2,1)S(1)} %collective-permute-done.43.refs_5_), channel_id=1, source_target_pairs={{0,2},{1,31},{2,4},{3,1},{4,6},{5,3},{6,8},{7,5},{8,10},{9,7},{10,... | collective-permute-start | bytes 1425416 | tf_op jit(solution)/shard_map/ppermute | solution.py:39
  244.9 14.1 %collective-permute-start.44 = (bf16[64,3712]{1,0:T(8,128)(2,1)S(1)}, bf16[64,3712]{1,0:T(8,128)(2,1)S(1)}, u32[]{:S(2)}, u32[]{:S(2)}) collective-permute-start(bf16[64,3712]{1,0:T(8,128)(2,1)S(1)} %collective-permute-done.42.refs_4_), channel_id=1, source_target_pairs={{0,2},{1,31},{2,4},{3,1},{4,6},{5,3},{6,8},{7,5},{8,10},{9,7},{10,... | collective-permute-start | bytes 1425416 | tf_op jit(solution)/shard_map/ppermute | solution.py:39
  259.0 12.8 %collective-permute-start.46 = (bf16[64,3712]{1,0:T(8,128)(2,1)S(1)}, bf16[64,3712]{1,0:T(8,128)(2,1)S(1)}, u32[]{:S(2)}, u32[]{:S(2)}) collective-permute-start(bf16[64,3712]{1,0:T(8,128)(2,1)S(1)} %collective-permute-done.44.refs_0_), channel_id=1, source_target_pairs={{0,2},{1,31},{2,4},{3,1},{4,6},{5,3},{6,8},{7,5},{8,10},{9,7},{10,... | collective-permute-start | bytes 1425416 | tf_op jit(solution)/shard_map/ppermute | solution.py:39
  266.8 12.3 %collective-permute-start.49 = (bf16[48,3712]{1,0:T(8,128)(2,1)S(1)}, bf16[48,3712]{1,0:T(8,128)(2,1)S(1)}, u32[]{:S(2)}, u32[]{:S(2)}) collective-permute-start(bf16[48,3712]{1,0:T(8,128)(2,1)S(1)} %slice.125), channel_id=1, source_target_pairs={{0,2},{1,31},{2,4},{3,1},{4,6},{5,3},{6,8},{7,5},{8,10},{9,7},{10,... | collective-permute-start | bytes 1069064 | tf_op jit(solution)/shard_map/ppermute | solution.py:39
  281.0 12.0 %collective-permute-start.50 = (bf16[48,3712]{1,0:T(8,128)(2,1)S(1)}, bf16[48,3712]{1,0:T(8,128)(2,1)S(1)}, u32[]{:S(2)}, u32[]{:S(2)}) collective-permute-start(bf16[48,3712]{1,0:T(8,128)(2,1)S(1)} %collective-permute-done.48.refs_0_), channel_id=1, source_target_pairs={{0,2},{1,31},{2,4},{3,1},{4,6},{5,3},{6,8},{7,5},{8,10},{9,7},{10,... | collective-permute-start | bytes 1069064 | tf_op jit(solution)/shard_map/ppermute | solution.py:39
  287.5 12.5 %collective-permute-start.55 = (bf16[24,3712]{1,0:T(8,128)(2,1)S(1)}, bf16[24,3712]{1,0:T(8,128)(2,1)S(1)}, u32[]{:S(2)}, u32[]{:S(2)}) collective-permute-start(bf16[24,3712]{1,0:T(8,128)(2,1)S(1)} %slice.127), channel_id=1, source_target_pairs={{1,29},{2,6},{5,1},{6,10},{9,5},{10,14},{13,9},{14,18},{17,13},{18... | collective-permute-start | bytes 534536 | tf_op jit(solution)/shard_map/ppermute | solution.py:39
  343.2 11.6 %collective-permute-start.68 = (bf16[64,3584]{1,0:T(8,128)(2,1)S(1)}, bf16[64,3584]{1,0:T(8,128)(2,1)S(1)}, u32[]{:S(2)}, u32[]{:S(2)}) collective-permute-start(bf16[64,3584]{1,0:T(8,128)(2,1)S(1)} %add_convert_fusion.4), channel_id=1, source_target_pairs={{2,0},{31,1},{4,2},{1,3},{6,4},{3,5},{8,6},{5,7},{10,8},{7,9},{12,... | collective-permute-start | bytes 1376264 | tf_op jit(solution)/shard_map/ppermute | solution.py:39
  387.3 13.9 %collective-permute-start.72 = (bf16[2,32,3584]{2,1,0:T(8,128)(2,1)S(1)}, bf16[2,32,3584]{2,1,0:T(8,128)(2,1)S(1)}, u32[]{:S(2)}, u32[]{:S(2)}) collective-permute-start(bf16[2,32,3584]{2,1,0:T(8,128)(2,1)S(1)} %slice.129), channel_id=1, source_target_pairs={{0,1},{1,0},{2,3},{3,2},{4,5},{5,4},{6,7},{7,6},{8,9},{9,8},{10,11... | collective-permute-start | bytes 1376264 | tf_op jit(solution)/shard_map/ppermute | solution.py:24
  (84 other events, 1108.3 us)
